TPU v7x, 256 devices: a whole 4x4x8 slice. The times are simulated.
256 devices in a mesh: seq: 32 (over z, y), tp: 8 (over x, core).
Axes of the slice: x: 4, y: 4, z: 8, core: 2. Of those that a mesh axis runs over, the one named last changes fastest.
Arguments:
- queries: bfloat16 [1024, 8192], P('seq', 'tp'), may hold values from -6 to 6
- prefix_keys: bfloat16 [32768, 1024], P('seq', 'tp'), may hold values from -10 to 10
- prefix_values: bfloat16 [32768, 1024], P('seq', 'tp'), may hold values from -6 to 6
- new_keys: bfloat16 [1024, 1024], P('seq', 'tp'), may hold values from -10 to 10
- new_values: bfloat16 [1024, 1024], P('seq', 'tp'), may hold values from -6 to 6
- cache_keys: bfloat16 [128, 512, 1024], P('seq', None, 'tp'), may hold values from -14 to 14
- cache_values: bfloat16 [128, 512, 1024], P('seq', None, 'tp'), may hold values from -6 to 6
- row_request: int32 [1024], P('seq'), may hold values from 0 to 127, as said below
- cache_lengths: int32 [128], P('seq'), may hold values from 1 to 512
- out_weight: bfloat16 [8192, 8192], P('tp', 'seq'), may hold values from -0.25 to 0.25
Outputs:
- projected: bfloat16 [1024, 8192], P('tp', 'seq')
Inputs may be any that keep to these rules, and one draw needn't show every extreme that they name: `row_request`: the rows of one request stand together on the index of seq that owns the request (requests s * 4 to s * 4 + 3 own rows s * 32 to s * 32 + 31), in order of position; each owner's first row belongs to its first request and its last row to its last.
All inputs are finite; a program needn't handle non-finite values.
Results may differ from a plain program's by a relative error of at most 0.019.
Values may be sent and summed in bfloat16 or wider, within the bound.
A program may use at most 320 MiB of HBM per device.

v0:
```python
import math

import jax
import jax.numpy as jnp
from jax import lax
from jax.sharding import PartitionSpec as P

HD = 128


def body(
    queries,
    prefix_keys,
    prefix_values,
    new_keys,
    new_values,
    cache_keys,
    cache_values,
    row_request,
    cache_lengths,
    out_weight,
):
    inv_root = 1.0 / math.sqrt(HD)
    own_rows = queries.shape[0]
    head_groups = prefix_keys.shape[1] // HD
    heads_here = queries.shape[1] // HD
    per_group = heads_here // head_groups
    prefix_rows = prefix_keys.shape[0]
    req_here = cache_keys.shape[0]
    request_slot_count = cache_keys.shape[1]
    owner_idx = lax.axis_index("seq")
    own_query = queries.reshape(own_rows, head_groups, per_group, HD)
    req_local = row_request - owner_idx * req_here
    suffix_keys = cache_keys.reshape(req_here, request_slot_count, head_groups, HD)
    suf_values = cache_values.reshape(req_here, request_slot_count, head_groups, HD)
    cache_scores = (
        jnp.einsum("rgqd,jkgd->rgqjk", own_query, suffix_keys, preferred_element_type=jnp.float32)
        * inv_root
    )
    slot_index = jnp.arange(request_slot_count, dtype=jnp.int32)
    req_index = jnp.arange(req_here, dtype=jnp.int32)
    usable = (req_local[:, None, None] == req_index[None, :, None]) & (
        slot_index[None, None, :] < cache_lengths[None, :, None]
    )
    cache_scores = jnp.where(usable[:, None, None], cache_scores, -jnp.inf)
    row_keys = new_keys.reshape(own_rows, head_groups, HD)
    row_values = new_values.reshape(own_rows, head_groups, HD)
    new_scores = (
        jnp.einsum("rgqd,sgd->rgqs", own_query, row_keys, preferred_element_type=jnp.float32)
        * inv_root
    )
    positions = jnp.arange(own_rows, dtype=jnp.int32)
    visible = (req_local[:, None] == req_local[None, :]) & (
        positions[None, :] <= positions[:, None]
    )
    new_scores = jnp.where(visible[:, None, None], new_scores, -jnp.inf)
    suf_max = jnp.maximum(cache_scores.max((3, 4)), new_scores.max(3))
    cache_exps = jnp.exp(cache_scores - suf_max[..., None, None])
    new_exps = jnp.exp(new_scores - suf_max[..., None])
    suf_totals = cache_exps.sum((3, 4)) + new_exps.sum(3)
    suf_out = jnp.einsum(
        "rgqjk,jkgd->rgqd",
        cache_exps.astype(jnp.bfloat16),
        suf_values,
        preferred_element_type=jnp.float32,
    )
    suf_out = suf_out + jnp.einsum(
        "rgqs,sgd->rgqd",
        new_exps.astype(jnp.bfloat16),
        row_values,
        preferred_element_type=jnp.float32,
    )
    all_queries = lax.all_gather(queries, "seq", axis=0, tiled=True)
    all_rows = all_queries.shape[0]
    block_rows = math.gcd(all_rows, 512)
    block_count = all_rows // block_rows
    pre_keys = prefix_keys.reshape(prefix_rows, head_groups, HD)
    prefix_value_rows = prefix_values.reshape(prefix_rows, head_groups, HD)

    def prefix_key_block(query_block):
        query_block = query_block.reshape(block_rows, head_groups, per_group, HD)
        pre_scores = (
            jnp.einsum("rgqd,kgd->rgqk", query_block, pre_keys, preferred_element_type=jnp.float32)
            * inv_root
        )
        row_max = pre_scores.max(3)
        pre_exps = jnp.exp(pre_scores - row_max[..., None])
        block_total = pre_exps.sum(3)
        summed = jnp.einsum(
            "rgqk,kgd->rgqd",
            pre_exps.astype(jnp.bfloat16),
            prefix_value_rows,
            preferred_element_type=jnp.float32,
        )
        return (
            (summed / block_total[..., None]).astype(jnp.bfloat16),
            row_max + jnp.log(block_total),
        )

    pre_out, pre_lse = lax.map(
        prefix_key_block, all_queries.reshape(block_count, block_rows, heads_here * HD)
    )
    pre_out = pre_out.reshape(all_rows, head_groups, per_group, HD)
    pre_lse = pre_lse.reshape(all_rows, head_groups, per_group)
    recv_out = lax.all_to_all(pre_out, "seq", split_axis=0, concat_axis=0, tiled=True)
    recv_lse = lax.all_to_all(pre_lse, "seq", split_axis=0, concat_axis=0, tiled=True)
    shards = all_rows // own_rows
    recv_out = recv_out.reshape(shards, own_rows, head_groups, per_group, HD)
    recv_lse = recv_lse.reshape(shards, own_rows, head_groups, per_group)
    top = jnp.maximum(recv_lse.max(0), suf_max)
    recv_w = jnp.exp(recv_lse - top)
    own_w = jnp.exp(suf_max - top)
    totals = recv_w.sum(0) + own_w * suf_totals
    summed = (
        jnp.einsum("srgq,srgqd->rgqd", recv_w, recv_out.astype(jnp.float32))
        + own_w[..., None] * suf_out
    )
    attended = (summed / totals[..., None]).astype(jnp.bfloat16).reshape(own_rows, heads_here * HD)
    gathered = lax.all_gather(attended, "seq", axis=0, tiled=True)
    return lax.psum_scatter(
        jnp.dot(gathered, out_weight, preferred_element_type=jnp.float32).astype(jnp.bfloat16),
        "tp",
        scatter_dimension=0,
        tiled=True,
    )


def solution(mesh):
    in_specs = (
        P("seq", "tp"),
        P("seq", "tp"),
        P("seq", "tp"),
        P("seq", "tp"),
        P("seq", "tp"),
        P("seq", None, "tp"),
        P("seq", None, "tp"),
        P("seq"),
        P("seq"),
        P("tp", "seq"),
    )
    out_specs = P("tp", "seq")
    return jax.shard_map(body, mesh=mesh, in_specs=in_specs, out_specs=out_specs, check_vma=False)
```

profile of v0, /device:TPU:1, one launch (start us, length us, event | category | flops | bytes accessed | tf_op | source)
XLA Modules:
  0.0 302.5 jit_solution(14642647473115784559)
XLA Ops:
  6.5 0.7 all-gather.3.cloned.1.call-update
  7.3 80.5 %all-gather.3.cloned.1.call-done = bf16[1024,1024]{1,0:T(8,128)(2,1)} async-done(((bf16[32,1024]{1,0:T(8,128)(2,1)}), bf16[1024,1024]{1,0:T(8,128)(2,1)}) %all-gather.3.cloned.1.call-update) | async-done | bytes 2097168 | tf_op jit(solution)/shard_map/all_gather | solution.py:73
  87.8 26.7 %while.12 = (s32[]{:T(128)}, bf16[2,512,1,8,128]{4,3,1,0,2:T(8,128)(2,1)}, f32[2,512,1,8]{1,3,2,0:T(8,128)S(1)}, bf16[2,512,1024]{2,1,0:T(8,128)(2,1)}, bf16[102...) while((s32[]{:T(128)}, bf16[2,512,1,8,128]{4,3,1,0,2:T(8,128)(2,1)}, ...), condition=%wide.region_3.4_spmd, body=%wide.region_0.0_spmd.sunk | while | flops 2182082560 | bytes 61473420 | solution.py:100
  87.8 1.3 constant_dynamic-slice_fusion.2
  89.2 0.5 copy.135
  89.7 2.4 bitcast_reduce_fusion.3
  92.2 3.7 %fusion.65 = f32[512,8]{0,1:T(8,128)S(1)} fusion(f32[512,8,1024]{2,0,1:T(8,128)S(1)} %get-tuple-element.137, f32[512,8]{0,1:T(8,128)S(1)} %get-tuple-element.138), kind=kLoop, calls=%fused_computation.3.clone.1 | loop fusion | flops 12578816 | bytes 16809984 | tf_op jit(solution)/shard_map/while/body/eval_jaxpr/reduce_sum | solution.py:88
  95.9 3.6 %fusion.66 = bf16[1,512,1,8,128]{4,1,3,2,0:T(8,128)(2,1)S(1)} fusion(f32[512,8,1024]{2,0,1:T(8,128)S(1)} %get-tuple-element.137, f32[512,8]{0,1:T(8,128)S(1)} %get-tuple-element.138, f32[512,8]{0,1:T(8,128)S(1)} %fusion.65, bf16[1024,1,128]{2,0,1:T(8,128)(2,1)S(1)} %copy-done.13), kind=kOutput, calls=%fused_computation.11.clone.1 | convolution fusion | flops 1087373312 | bytes 18120704 | tf_op jit(solution)/shard_map/while/body/eval_jaxpr/rgqk,kgd->rgqd/dot_general | solution.py:89
  99.5 1.7 copy_dynamic-update-slice_fusion.2
  101.2 1.3 constant_dynamic-slice_fusion.2
  102.5 0.5 copy.135
  103.1 2.4 bitcast_reduce_fusion.3
  105.5 3.7 %fusion.65 = f32[512,8]{0,1:T(8,128)S(1)} fusion(f32[512,8,1024]{2,0,1:T(8,128)S(1)} %get-tuple-element.137, f32[512,8]{0,1:T(8,128)S(1)} %get-tuple-element.138), kind=kLoop, calls=%fused_computation.3.clone.1 | loop fusion | flops 12578816 | bytes 16809984 | tf_op jit(solution)/shard_map/while/body/eval_jaxpr/reduce_sum | solution.py:88
  109.3 3.6 %fusion.66 = bf16[1,512,1,8,128]{4,1,3,2,0:T(8,128)(2,1)S(1)} fusion(f32[512,8,1024]{2,0,1:T(8,128)S(1)} %get-tuple-element.137, f32[512,8]{0,1:T(8,128)S(1)} %get-tuple-element.138, f32[512,8]{0,1:T(8,128)S(1)} %fusion.65, bf16[1024,1,128]{2,0,1:T(8,128)(2,1)S(1)} %copy-done.13), kind=kOutput, calls=%fused_computation.11.clone.1 | convolution fusion | flops 1087373312 | bytes 18120704 | tf_op jit(solution)/shard_map/while/body/eval_jaxpr/rgqk,kgd->rgqd/dot_general | solution.py:89
  112.9 1.7 copy_dynamic-update-slice_fusion.2
  114.5 0.5 broadcast.113
  115.0 0.6 reduce.8
  115.7 0.2 copy.131
  115.9 0.3 reshape.331
  116.2 13.5 %all_to_all.10 = f32[32,1,256]{2,1,0:T(1,128)S(1)} all-to-all(f32[32,1,256]{2,1,0:T(1,128)S(1)} %reshape.331), channel_id=1, replica_groups=mesh['seq'=32,'tp'=8] {'seq'}, dimensions={0} | all-to-all | bytes 65536 | tf_op jit(solution)/shard_map/all_to_all | solution.py:106
  129.7 4.9 %all-to-all-start.1 = ((bf16[1024,1,8,128]{3,2,1,0:T(8,128)(2,1)}), bf16[1024,1,8,128]{3,2,1,0:T(8,128)(2,1)}, u32[]{:S(2)}, u32[]{:S(2)}) async-start(bf16[1024,1,8,128]{3,2,1,0:T(8,128)(2,1)} %bitcast.31), calls=%async_computation.1 | async-start | bytes 4194304 | tf_op jit(solution)/shard_map/all_to_all | solution.py:105
  134.7 0.0 all-gather.5.cloned.1.call-start
  134.8 0.1 iota_compare_fusion.1
  134.8 0.1 fusion.45
  134.9 0.1 broadcast_and_fusion
  135.0 0.2 fusion.50
  135.3 0.5 fusion.49
  135.8 0.7 reduce.9
  136.5 0.9 reshape.332
  137.4 0.1 bitcast_reduce_fusion.1
  137.5 0.1 copy.91
  137.5 0.6 fusion.48
  138.1 0.1 copy.92
  138.2 0.5 copy-done.7
  138.7 0.1 exponential_reduce_fusion
  138.8 0.7 copy.98
  139.5 0.1 fusion.36
  139.6 1.0 copy.102
  140.6 0.8 fusion.37
  141.4 1.1 fusion.20
  142.6 0.5 convolution_bitcast_fusion
  143.2 35.7 %all-to-all-done.1 = bf16[1024,1,8,128]{3,2,1,0:T(8,128)(2,1)} async-done(((bf16[1024,1,8,128]{3,2,1,0:T(8,128)(2,1)}), bf16[1024,1,8,128]{3,2,1,0:T(8,128)(2,1)}, u32[]{:S(2)}, u32[]{:S(2)}) %all-to-all-start.1) | async-done | bytes 2097184 | tf_op jit(solution)/shard_map/all_to_all | solution.py:105
  178.9 2.9 fusion.18
  181.8 0.2 fusion.28
  182.1 0.6 copy.130
  182.8 77.7 %all-gather.5.cloned.1.call-done = bf16[1024,1024]{1,0:T(8,128)(2,1)} async-done(((bf16[32,1024]{1,0:T(8,128)(2,1)}), bf16[1024,1024]{1,0:T(8,128)(2,1)}) %all-gather.5.cloned.1.call-update) | async-done | bytes 2097168 | tf_op jit(solution)/shard_map/all_gather | solution.py:119
  260.5 3.1 %convolution_convert_fusion = bf16[1024,256]{1,0:T(8,128)(2,1)} fusion(bf16[1024,1024]{1,0:T(8,128)(2,1)} %all-gather.5.cloned.1.call-done, bf16[1024,256]{1,0:T(8,128)(2,1)S(1)} %copy-done.12), kind=kOutput, calls=%fused_computation.25 | convolution fusion | flops 537133056 | bytes 3145728 | tf_op jit(solution)/shard_map/dot_general | solution.py:121
  263.6 32.3 %reduce-scatter.2.cloned.1.call-done = bf16[128,256]{1,0:T(8,128)(2,1)} async-done(((bf16[1024,256]{1,0:T(8,128)(2,1)}), bf16[128,256]{1,0:T(8,128)(2,1)}) %reduce-scatter.2.cloned.1.call-update) | async-done | bytes 65552 | tf_op jit(solution)/shard_map/reduce_scatter | solution.py:120
  (47 shorter events, 0.2 us)
Async XLA Ops:
  6.5 128.7 %copy-start = (bf16[4,512,128]{2,1,0:T(8,128)(2,1)S(1)}, bf16[4,512,128]{2,1,0:T(8,128)(2,1)}, u32[]{:S(2)}) copy-start(bf16[4,512,128]{2,1,0:T(8,128)(2,1)} %param.17) | copy-start | bytes 1572868
  6.5 81.3 %all-gather.3.cloned.1.call-start = ((), (), s32[]{:S(2)}) async-start(), calls=%async_computation.3 | async-start | bytes 2162688 | tf_op jit(solution)/shard_map/all_gather | solution.py:73
  87.8 1.9 copy-start.1
  92.2 3.7 %copy-start.13 = (bf16[1024,1,128]{2,0,1:T(8,128)(2,1)S(1)}, bf16[1024,1,128]{2,0,1:T(8,128)(2,1)}, u32[]{:S(2)}) copy-start(bf16[1024,1,128]{2,0,1:T(8,128)(2,1)} %get-tuple-element.158) | copy-start | bytes 786436 | tf_op jit(solution)/shard_map/while
  101.2 1.9 copy-start.1
  105.5 3.7 %copy-start.13 = (bf16[1024,1,128]{2,0,1:T(8,128)(2,1)S(1)}, bf16[1024,1,128]{2,0,1:T(8,128)(2,1)}, u32[]{:S(2)}) copy-start(bf16[1024,1,128]{2,0,1:T(8,128)(2,1)} %get-tuple-element.158) | copy-start | bytes 786436 | tf_op jit(solution)/shard_map/while
  129.7 5.0 %copy-start.15 = (s32[32]{0:T(128)S(1)}, s32[32]{0:T(128)}, u32[]{:S(2)}) copy-start(s32[32]{0:T(128)} %param.19) | copy-start | bytes 388
  129.7 5.0 %copy-start.11 = (s32[4]{0:T(128)S(1)}, s32[4]{0:T(128)}, u32[]{:S(2)}) copy-start(s32[4]{0:T(128)} %param.20) | copy-start | bytes 52
  129.7 5.3 %copy-start.2 = (bf16[32,1024]{1,0:T(8,128)(2,1)S(1)}, bf16[32,1024]{1,0:T(8,128)(2,1)}, u32[]{:S(2)}) copy-start(bf16[32,1024]{1,0:T(8,128)(2,1)} %param.12) | copy-start | bytes 196612
  129.7 5.3 %copy-start.10 = (bf16[32,128]{1,0:T(8,128)(2,1)S(1)}, bf16[32,128]{1,0:T(8,128)(2,1)}, u32[]{:S(2)}) copy-start(bf16[32,128]{1,0:T(8,128)(2,1)} %param.15) | copy-start | bytes 24580
  129.7 49.1 %all-to-all-start.1 = ((bf16[1024,1,8,128]{3,2,1,0:T(8,128)(2,1)}), bf16[1024,1,8,128]{3,2,1,0:T(8,128)(2,1)}, u32[]{:S(2)}, u32[]{:S(2)}) async-start(bf16[1024,1,8,128]{3,2,1,0:T(8,128)(2,1)} %bitcast.31), calls=%async_computation.1 | async-start | bytes 4194304 | tf_op jit(solution)/shard_map/all_to_all | solution.py:105
  134.7 125.8 %all-gather.5.cloned.1.call-start = ((), (), s32[]{:S(2)}) async-start(), calls=%async_computation.4 | async-start | bytes 2162688 | tf_op jit(solution)/shard_map/all_gather | solution.py:119
  138.1 0.6 copy-start.7
  139.6 3.0 copy-start.5
  139.6 3.0 copy-start.8
  139.6 3.0 copy-start.9
  139.6 3.0 copy-start.3
  140.6 2.0 copy-start.6
  141.4 37.5 %copy-start.4 = (bf16[32,32,8,1]{0,3,2,1:T(2,128)(2,1)S(1)}, bf16[32,32,8,1]{0,3,2,1:T(2,128)(2,1)}, u32[]{:S(2)}) copy-start(bf16[32,32,8,1]{0,3,2,1:T(2,128)(2,1)} %copy.102) | copy-start | bytes 49156
  143.1 38.7 %copy-start.14 = (bf16[32,128]{1,0:T(8,128)(2,1)S(1)}, bf16[32,128]{1,0:T(8,128)(2,1)}, u32[]{:S(2)}) copy-start(bf16[32,128]{1,0:T(8,128)(2,1)} %param.16) | copy-start | bytes 24580
  143.1 117.4 %copy-start.12 = (bf16[1024,256]{1,0:T(8,128)(2,1)S(1)}, bf16[1024,256]{1,0:T(8,128)(2,1)}, u32[]{:S(2)}) copy-start(bf16[1024,256]{1,0:T(8,128)(2,1)} %param.21) | copy-start | bytes 1572868
  182.7 113.2 %reduce-scatter.2.cloned.1.call-start = ((), (), s32[]{:S(2)}) async-start(), calls=%async_computation.5 | async-start | bytes 589824 | tf_op jit(solution)/shard_map/reduce_scatter | solution.py:120
Sparse Core Ops, SparseCore 0:
  9.9 77.8 all-gather.2
  182.9 77.5 all-gather.4
  263.7 32.1 reduce-scatter.1
where the time goes:
time: 304 us; the launch traced here: 303 us
  waiting for transfers between devices  227 us (75%)
  matrix products  19.5 us (6%)
  blocking collectives  13.5 us (4%)
  between operations  13.4 us (4%)
  local copies, waits for them, and re-layouts  12 us (4%)
  other arithmetic  11.9 us (4%)
  starting transfers between devices  4.99 us (2%)
    all_gather x1, waiting for transfers between devices, body(): all_queries = lax.all_gather(queries, 'seq', axis=0, tiled=True)  80.5 us
    all_gather x1, waiting for transfers between devices, body(): gathered = lax.all_gather(attended, 'seq', axis=0, tiled=True)  77.7 us
    all_to_all x1, waiting for transfers between devices, body(): lax.all_to_all(pre_out, 'seq', split_axis=0, concat_axis=0, tiled=True)  35.7 us
    reduce_scatter x1, waiting for transfers between devices, body(): lax.psum_scatter(jnp.dot(gathered, out_weight, preferred_element_type=jnp...  32.3 us
    all_to_all x1, blocking collectives, body(): lax.all_to_all(pre_lse, 'seq', split_axis=0, concat_axis=0, tiled=True)  13.5 us
    reduce_sum x2, other arithmetic, prefix_key_block(): block_total = pre_exps.sum(3)  7.42 us
    dot_general x2, matrix products, prefix_key_block(): jnp.einsum('rgqk,kgd->rgqd', pre_exps.astype(jnp.bfloat16), prefix_value_...  7.12 us
  transfers between devices with their start and end apart: 4, of which 4 were waited for; matrix products, arithmetic and copies ran while one was open for 3% of the time, Pallas kernels for 0%

commit v1 on v0

v1 whole, which is shorter than its diff:
```python
import functools
import math

import jax
import jax.numpy as jnp
from jax import lax
from jax.experimental import pallas as pl
from jax.experimental.pallas import tpu as pltpu
from jax.sharding import PartitionSpec as P

HD = 128
QPG = 8
NY = 4
MESH = pl.DeviceIdType.MESH
SCALE2 = math.log2(math.e) / math.sqrt(HD)
LOG2E = math.log2(math.e)
LOW = -1e30
F32 = jnp.float32
BF16 = jnp.bfloat16


class Ring:
    def __init__(self, n, left, right, send_sem, recv_sem):
        self.n, self.left, self.right = n, left, right
        self.send_sem, self.recv_sem = send_sem, recv_sem
        self.last = n // 2

    def copy(self, way, k, src, dst):
        return pltpu.make_async_remote_copy(
            src_ref=src,
            dst_ref=dst,
            send_sem=self.send_sem.at[way, k - 1],
            recv_sem=self.recv_sem.at[way, k - 1],
            device_id=self.right if way == 0 else self.left,
            device_id_type=MESH,
        )


def kernel(
    nz,
    q_ref,
    pk_ref,
    pv_ref,
    nk_ref,
    nv_ref,
    ck_ref,
    cv_ref,
    rr_ref,
    cl_ref,
    w_ref,
    out_ref,
    kbuf,
    vbuf,
    qbuf,
    wbuf,
    ckb,
    cvb,
    nkb,
    nvb,
    acc,
    mst,
    osend,
    orecv,
    lsend,
    lrecv,
    att,
    psend,
    precv,
    fsend,
    frecv,
    loc_sem,
    qs,
    qr,
    ks,
    kr,
    ws,
    wr,
    os_,
    or_,
    ls,
    lr,
    as_,
    ar,
    ps,
    pr,
    fs,
    fr,
):
    nt = nz
    rows = q_ref.shape[0]
    keys = pk_ref.shape[0]
    reqs, slots = ck_ref.shape[0], ck_ref.shape[1]
    s_idx = lax.axis_index("seq")
    t = lax.axis_index("tp")
    z = s_idx // NY
    y = s_idx % NY

    def at_z(v):
        return (lax.rem(v + 2 * nz, nz) * NY + y, t)

    def at_y(v):
        return (z * NY + lax.rem(v + 2 * NY, NY), t)

    def at_t(v):
        return (s_idx, lax.rem(v + 2 * nt, nt))

    barrier = pltpu.get_barrier_semaphore()
    for i in range(1, nz):
        pl.semaphore_signal(barrier, inc=1, device_id=at_z(z + i), device_id_type=MESH)
    for i in range(1, NY):
        pl.semaphore_signal(barrier, inc=1, device_id=at_y(y + i), device_id_type=MESH)
    for i in range(1, nt):
        pl.semaphore_signal(barrier, inc=1, device_id=at_t(t + i), device_id_type=MESH)

    local = [
        pltpu.make_async_copy(q_ref, qbuf.at[0], loc_sem.at[0]),
        pltpu.make_async_copy(ck_ref, ckb, loc_sem.at[1]),
        pltpu.make_async_copy(cv_ref, cvb, loc_sem.at[2]),
        pltpu.make_async_copy(nk_ref, nkb.at[pl.ds(0, rows)], loc_sem.at[3]),
        pltpu.make_async_copy(nv_ref, nvb.at[pl.ds(0, rows)], loc_sem.at[4]),
        pltpu.make_async_copy(pk_ref, kbuf.at[0], loc_sem.at[5]),
        pltpu.make_async_copy(pv_ref, vbuf.at[0], loc_sem.at[6]),
        pltpu.make_async_copy(w_ref, wbuf.at[y], loc_sem.at[7]),
    ]
    for c in local:
        c.start()
    pl.semaphore_wait(barrier, nz + NY + nt - 3)

    half = rows // 2
    zl, zr = at_z(z - 1), at_z(z + 1)
    yl, yr = at_y(y - 1), at_y(y + 1)
    qring = Ring(nz, zl, zr, qs, qr)
    last = nz // 2
    halves = (pl.ds(0, half), pl.ds(half, half))

    def q_slot(way, k):
        return 2 * k - 1 if (way == 0 or k == last) else 2 * k

    def q_copy(way, k):
        dst = qbuf.at[q_slot(way, k)]
        if k == 1:
            src = q_ref
        else:
            src = qbuf.at[q_slot(way, k - 1)]
        if k == last:
            src, dst = src.at[halves[way]], dst.at[halves[way]]
        return qring.copy(way, k, src, dst)

    for way in range(2):
        q_copy(way, 1).start()

    def remote(src, dst, ssem, rsem, dev):
        return pltpu.make_async_remote_copy(
            src_ref=src,
            dst_ref=dst,
            send_sem=ssem,
            recv_sem=rsem,
            device_id=dev,
            device_id_type=MESH,
        )

    k_right = remote(pk_ref, kbuf.at[1], ks.at[0], kr.at[0], yr)
    v_right = remote(pv_ref, vbuf.at[1], ks.at[1], kr.at[1], yr)
    k_left = remote(pk_ref, kbuf.at[2], ks.at[2], kr.at[2], yl)
    v_left = remote(pv_ref, vbuf.at[2], ks.at[3], kr.at[3], yl)
    k_fwd = remote(kbuf.at[1], kbuf.at[3], ks.at[4], kr.at[4], yr)
    v_fwd = remote(vbuf.at[2], vbuf.at[3], ks.at[5], kr.at[5], yl)
    k_right.start()
    k_left.start()
    v_right.start()
    v_left.start()

    pad = nkb.shape[0]
    nkb[pl.ds(rows, pad - rows), :] = jnp.zeros((pad - rows, HD), BF16)
    nvb[pl.ds(rows, pad - rows), :] = jnp.zeros((pad - rows, HD), BF16)
    for c in local[:5]:
        c.wait()
    rr_lane = rr_ref[...]
    sub = lax.broadcasted_iota(jnp.int32, (rows, pad), 0)
    lane = lax.broadcasted_iota(jnp.int32, (rows, pad), 1)
    rr_all = jnp.broadcast_to(rr_lane, (rows, pad))
    rr_col = jnp.sum(jnp.where(sub == lane, rr_all, 0), axis=1, keepdims=True) - s_idx * reqs

    def queries_of(i):
        return jnp.concatenate(
            [qbuf[i, :, h * HD : (h + 1) * HD] for h in range(QPG)], axis=0
        )

    def scores(q, k):
        return lax.dot_general(q, k, (((1,), (1,)), ((), ())), preferred_element_type=F32)

    q_own = queries_of(0)
    parts = []
    slot_lane = lax.broadcasted_iota(jnp.int32, (rows, slots), 1)
    for j in range(reqs):
        ok = (rr_col == j) & (slot_lane < cl_ref[j])
        bias = jnp.where(ok, 0.0, LOW).astype(F32)
        parts.append(scores(q_own, ckb[j]) + jnp.concatenate([bias] * QPG, axis=0))
    ok = (rr_all - s_idx * reqs == rr_col) & (lane <= sub)
    bias = jnp.where(ok, 0.0, LOW).astype(F32)
    parts.append(scores(q_own, nkb[...]) + jnp.concatenate([bias] * QPG, axis=0))
    top = functools.reduce(jnp.maximum, [p.max(axis=1, keepdims=True) for p in parts])
    total = jnp.zeros((rows * QPG, 2 * HD), F32)
    for j, p in enumerate(parts):
        w = jnp.exp2((p - top) * SCALE2).astype(BF16)
        v = cvb[j] if j < reqs else nvb[...]
        vv = jnp.concatenate([v, jnp.ones_like(v)], axis=1)
        total = total + jnp.dot(w, vv, preferred_element_type=F32)
    acc[0] = total
    mst[0] = jnp.broadcast_to(top, (rows * QPG, HD))
    for i in range(1, nz):
        acc[i] = jnp.zeros((rows * QPG, 2 * HD), F32)
        mst[i] = jnp.full((rows * QPG, HD), LOW, F32)

    def flash(i, blk):
        q = queries_of(i)
        s = scores(q, kbuf[blk])
        chunks = [s[:, c * HD : (c + 1) * HD] for c in range(keys // HD)]
        m_old = mst[i]
        m_new = jnp.maximum(
            m_old, functools.reduce(jnp.maximum, chunks).max(axis=1, keepdims=True)
        )
        m2 = m_new * SCALE2
        w = jnp.concatenate(
            [jnp.exp2(c * SCALE2 - m2).astype(BF16) for c in chunks], axis=1
        )
        v = vbuf[blk]
        o = jnp.dot(w, jnp.concatenate([v, jnp.ones_like(v)], axis=1), preferred_element_type=F32)
        alpha = jnp.exp2(m_old * SCALE2 - m2)
        acc[i] = acc[i] * jnp.concatenate([alpha, alpha], axis=1) + o
        mst[i] = m_new

    for c in local[5:7]:
        c.wait()

    def first(p, carry):
        for k in range(1, last + 1):

            @pl.when(p == k - 1)
            def _(k=k):
                for way in range(2):
                    q_copy(way, k).wait_recv()
                    if k < last:
                        q_copy(way, k + 1).start()

        flash(2 * p, 0)
        flash(2 * p + 1, 0)
        return carry

    lax.fori_loop(0, last, first, 0)

    k_right.wait_recv()
    k_fwd.start()
    v_left.wait_recv()
    v_fwd.start()
    v_right.wait_recv()
    k_left.wait_recv()

    def middle(n, carry):
        p = lax.rem(n, last)
        blk = 1 + n // last
        flash(2 * p, blk)
        flash(2 * p + 1, blk)
        return carry

    lax.fori_loop(0, 2 * last, middle, 0)
    k_fwd.wait_recv()
    v_fwd.wait_recv()

    depth = w_ref.shape[0]
    whalf = (pl.ds(0, depth // 2), pl.ds(depth // 2, depth // 2))
    left_y = lax.rem(y + NY - 1, NY)
    right_y = lax.rem(y + 1, NY)
    w_right = remote(w_ref, wbuf.at[y], ws.at[0], wr.at[0], yr)
    w_left = remote(w_ref, wbuf.at[y], ws.at[1], wr.at[1], yl)
    w_fwd0 = remote(
        wbuf.at[left_y, whalf[0]], wbuf.at[left_y, whalf[0]], ws.at[2], wr.at[2], yr
    )
    w_fwd1 = remote(
        wbuf.at[right_y, whalf[1]], wbuf.at[right_y, whalf[1]], ws.at[3], wr.at[3], yl
    )
    w_right.start()
    w_left.start()

    lane8 = lax.broadcasted_iota(jnp.int32, (8, HD), 1)
    groups = rows // 8

    def o_copies(i):
        up = lax.rem(i, 2)
        off = ((i + 1) // 2) * (2 * up - 1)
        dev = at_z(z - off)
        return (
            remote(osend.at[i], orecv.at[i], os_.at[i], or_.at[i], dev),
            remote(lsend.at[i], lrecv.at[i], ls.at[i], lr.at[i], dev),
        )

    def finish(i):
        a = acc[i]
        l = a[:, HD:]
        osend[i] = (a[:, :HD] / l).astype(BF16)
        lse = mst[i] * SCALE2 + jnp.log(l) * LOG2E
        packed = jnp.zeros((8, HD), F32)
        for h in range(QPG):
            for g in range(groups):
                r0 = h * rows + g * 8
                packed = jnp.where(lane8 == g * 8 + h, lse[r0 : r0 + 8, :], packed)
        lsend[i] = packed

    def final(n, carry):
        p = last - 1 - n
        flash(2 * p, 3)
        flash(2 * p + 1, 3)
        finish(2 * p)
        finish(2 * p + 1)
        for c in o_copies(2 * p + 1):
            c.start()

        @pl.when(p > 0)
        def _():
            for c in o_copies(2 * p):
                c.start()

        return carry

    lax.fori_loop(0, last, final, 0)

    w_right.wait_recv()
    w_fwd0.start()
    w_left.wait_recv()
    w_fwd1.start()

    for i in range(nz - 1, 0, -1):
        for c in o_copies(i):
            c.wait_recv()

    lses = [lsend[0]] + [lrecv[i] for i in range(1, nz)]
    best = functools.reduce(jnp.maximum, lses)
    wts = [jnp.exp2(v - best) for v in lses]
    norm = functools.reduce(jnp.add, wts)
    wts = [v / norm for v in wts]
    for h in range(QPG):
        tot = jnp.zeros((rows, HD), F32)
        for i in range(nz):
            o = (osend if i == 0 else orecv)[i, h * rows : (h + 1) * rows, :].astype(F32)
            col = jnp.concatenate(
                [wts[i][:, g * 8 + h : g * 8 + h + 1] for g in range(groups)], axis=0
            )
            tot = tot + o * col
        att[z, :, h * HD : (h + 1) * HD] = tot.astype(BF16)

    aring = Ring(nz, zl, zr, as_, ar)

    def a_copy(way, k):
        origin = lax.rem(z + (1 - k if way == 0 else k - 1) + nz, nz)
        ref = att.at[origin]
        if k == last:
            ref = ref.at[halves[way]]
        return aring.copy(way, k, ref, ref)

    for way in range(2):
        a_copy(way, 1).start()
    for k in range(1, last + 1):
        for way in range(2):
            a_copy(way, k).wait_recv()
            if k < last:
                a_copy(way, k + 1).start()

    local[7].wait()
    w_fwd0.wait_recv()
    w_fwd1.wait_recv()
    cols = w_ref.shape[1]
    a_all = att[...].reshape(nz * rows, depth)
    for j in range(NY):
        pj = jnp.dot(a_all, wbuf[j], preferred_element_type=F32).astype(BF16)
        psend[:, :, j * cols : (j + 1) * cols] = pj.reshape(nz, rows, cols)

    def p_copy(e):
        dst_t = lax.rem(t + e, nt)
        return remote(psend.at[dst_t], precv.at[e], ps.at[e], pr.at[e], at_t(t + e))

    for e in range(1, nt):
        p_copy(e).start()
    tot = psend[t].astype(F32)
    for e in range(1, nt):
        p_copy(e).wait_recv()
        tot = tot + precv[e].astype(F32)
    tot = tot.astype(BF16)
    for j in range(NY):
        fsend[j] = tot[:, j * cols : (j + 1) * cols]

    def f_copy(e):
        dst_y = lax.rem(y + e, NY)
        return remote(fsend.at[dst_y], frecv.at[y], fs.at[e], fr.at[e], at_y(y + e))

    for e in range(1, NY):
        f_copy(e).start()
    frecv[y] = fsend[y]
    for e in range(1, NY):
        f_copy(e).wait_recv()
    out_ref[...] = frecv[...].reshape(NY * rows, cols)

    for way in range(2):
        for k in range(1, last + 1):
            q_copy(way, k).wait_send()
            a_copy(way, k).wait_send()
    for c in (k_right, v_right, k_left, v_left, k_fwd, v_fwd, w_right, w_left, w_fwd0, w_fwd1):
        c.wait_send()
    for i in range(1, nz):
        for c in o_copies(i):
            c.wait_send()
    for e in range(1, nt):
        p_copy(e).wait_send()
    for e in range(1, NY):
        f_copy(e).wait_send()


def body(nz, q, pk, pv, nk, nv, ck, cv, rr, cl, w):
    rows = q.shape[0]
    feat = q.shape[1]
    keys = pk.shape[0]
    reqs, slots = ck.shape[0], ck.shape[1]
    depth, cols = w.shape
    m = rows * QPG
    wide = NY * cols
    last = nz // 2
    vm = pltpu.VMEM
    dma = pltpu.SemaphoreType.DMA
    any_spec = pl.BlockSpec(memory_space=pl.ANY)
    vmem_spec = pl.BlockSpec(memory_space=pltpu.VMEM)
    smem_spec = pl.BlockSpec(memory_space=pltpu.SMEM)
    rr = jnp.pad(rr.reshape(1, rows), ((0, 0), (0, HD - rows)), constant_values=-1)
    return pl.pallas_call(
        functools.partial(kernel, nz),
        out_shape=jax.ShapeDtypeStruct((NY * rows, cols), BF16),
        in_specs=[any_spec] * 7 + [vmem_spec, smem_spec, any_spec],
        out_specs=vmem_spec,
        scratch_shapes=[
            vm((NY, keys, HD), BF16),
            vm((NY, keys, HD), BF16),
            vm((nz, rows, feat), BF16),
            vm((NY, depth, cols), BF16),
            vm((reqs, slots, HD), BF16),
            vm((reqs, slots, HD), BF16),
            vm((HD, HD), BF16),
            vm((HD, HD), BF16),
            vm((nz, m, 2 * HD), F32),
            vm((nz, m, HD), F32),
            vm((nz, m, HD), BF16),
            vm((nz, m, HD), BF16),
            vm((nz, 8, HD), F32),
            vm((nz, 8, HD), F32),
            vm((nz, rows, depth), BF16),
            vm((nz, rows, wide), BF16),
            vm((nz, rows, wide), BF16),
            vm((NY, rows, cols), BF16),
            vm((NY, rows, cols), BF16),
            dma((8,)),
            dma((2, last)),
            dma((2, last)),
            dma((6,)),
            dma((6,)),
            dma((4,)),
            dma((4,)),
            dma((nz,)),
            dma((nz,)),
            dma((nz,)),
            dma((nz,)),
            dma((2, last)),
            dma((2, last)),
            dma((nz,)),
            dma((nz,)),
            dma((NY,)),
            dma((NY,)),
        ],
        compiler_params=pltpu.CompilerParams(
            collective_id=0, has_side_effects=True, vmem_limit_bytes=48 * 1024 * 1024
        ),
    )(q, pk, pv, nk, nv, ck, cv, rr, cl, w)


def solution(mesh):
    nz = mesh.shape["seq"] // NY
    in_specs = (
        P("seq", "tp"),
        P("seq", "tp"),
        P("seq", "tp"),
        P("seq", "tp"),
        P("seq", "tp"),
        P("seq", None, "tp"),
        P("seq", None, "tp"),
        P("seq"),
        P("seq"),
        P("tp", "seq"),
    )
    return jax.shard_map(
        functools.partial(body, nz),
        mesh=mesh,
        in_specs=in_specs,
        out_specs=P("tp", "seq"),
        check_vma=False,
    )
```

time: 304 us -> 83.4 us (0.27)
  waiting for transfers between devices: 227 us -> 0 us
  Pallas kernels: 0 us -> 73.7 us
  matrix products: 19.5 us -> 0 us
  blocking collectives: 13.5 us -> 0 us
  between operations: 13.4 us -> 0.02 us
  other arithmetic: 11.9 us -> 0 us
  starting transfers between devices: 4.99 us -> 0 us
    all_gather x2 -> x0, waiting for transfers between devices: 158 us -> none  [the longest x1 80.5 us: body(): all_queries = lax.all_gather(queries, 'seq', axis=0, tiled=True)]
    pallas_call x0 -> x1, Pallas kernels: none -> 73.7 us  [body(): pl.pallas_call(functools.partial(kernel, nz), out_shape=jax.ShapeDtypeStr...]
    all_to_all x1 -> x0, waiting for transfers between devices: 35.7 us -> none  [body(): lax.all_to_all(pre_out, 'seq', split_axis=0, concat_axis=0, tiled=True)]
    reduce_scatter x1 -> x0, waiting for transfers between devices: 32.3 us -> none  [body(): lax.psum_scatter(jnp.dot(gathered, out_weight, preferred_element_type=jnp...]
    dot_general x10 -> x0, matrix products: 19.5 us -> none  [the longest x2 7.12 us: prefix_key_block(): jnp.einsum('rgqk,kgd->rgqd', pre_exps.astype(jnp.bfloat16), prefix_value_...]
    all_to_all x1 -> x0, blocking collectives: 13.5 us -> none  [body(): lax.all_to_all(pre_lse, 'seq', split_axis=0, concat_axis=0, tiled=True)]
    reduce_sum x5 -> x0, other arithmetic: 9.46 us -> none  [the longest x2 7.42 us: prefix_key_block(): block_total = pre_exps.sum(3)]
    unnamed x32 -> x21, local copies, waits for them, and re-layouts: 2.57 us -> 9.19 us
  transfers between devices with their start and end apart: 4 -> 0, of which waited for: 4 -> 0; matrix products, arithmetic and copies ran while one was open for 3% -> 0% of each run, Pallas kernels for 0% -> 0%
where the time goes in v1:
time: 83.4 us; the launch traced here: 82.9 us
  Pallas kernels  73.7 us (88%)
  local copies, waits for them, and re-layouts  9.19 us (11%)
    pallas_call x1, Pallas kernels, body(): pl.pallas_call(functools.partial(kernel, nz), out_shape=jax.ShapeDtypeStr...  73.7 us
    unnamed x21, local copies, waits for them, and re-layouts  9.19 us

profile of v1, /device:TPU:1, one launch (start us, length us, event | category | flops | bytes accessed | tf_op | source)
XLA Modules:
  0.0 82.9 jit_solution(6560596495690580046)
XLA Ops:
  0.0 0.0 copy-start.9
  0.0 0.7 copy-done.9
  0.7 0.0 copy-start.8
  0.7 0.6 copy-done.8
  1.3 0.0 copy-start
  1.3 1.0 %copy-done = bf16[4,512,128]{2,1,0:T(8,128)(2,1)S(1)} copy-done((bf16[4,512,128]{2,1,0:T(8,128)(2,1)S(1)}, bf16[4,512,128]{2,1,0:T(8,128)(2,1)}, u32[]{:S(2)}) %copy-start) | copy-done | bytes 524312
  2.4 0.0 copy-start.1
  2.4 1.0 %copy-done.1 = bf16[4,512,128]{2,1,0:T(8,128)(2,1)S(1)} copy-done((bf16[4,512,128]{2,1,0:T(8,128)(2,1)S(1)}, bf16[4,512,128]{2,1,0:T(8,128)(2,1)}, u32[]{:S(2)}) %copy-start.1) | copy-done | bytes 524312
  3.4 0.0 copy-start.2
  3.4 1.0 %copy-done.2 = bf16[1024,256]{1,0:T(8,128)(2,1)S(1)} copy-done((bf16[1024,256]{1,0:T(8,128)(2,1)S(1)}, bf16[1024,256]{1,0:T(8,128)(2,1)}, u32[]{:S(2)}) %copy-start.2) | copy-done | bytes 524312
  4.4 0.0 copy-start.3
  4.4 0.9 %copy-done.3 = bf16[1024,128]{1,0:T(8,128)(2,1)S(1)} copy-done((bf16[1024,128]{1,0:T(8,128)(2,1)S(1)}, bf16[1024,128]{1,0:T(8,128)(2,1)}, u32[]{:S(2)}) %copy-start.3) | copy-done | bytes 262168
  5.4 0.0 copy-start.4
  5.4 0.9 %copy-done.4 = bf16[1024,128]{1,0:T(8,128)(2,1)S(1)} copy-done((bf16[1024,128]{1,0:T(8,128)(2,1)S(1)}, bf16[1024,128]{1,0:T(8,128)(2,1)}, u32[]{:S(2)}) %copy-start.4) | copy-done | bytes 262168
  6.3 0.0 copy-start.5
  6.3 0.8 %copy-done.5 = bf16[32,1024]{1,0:T(8,128)(2,1)S(1)} copy-done((bf16[32,1024]{1,0:T(8,128)(2,1)S(1)}, bf16[32,1024]{1,0:T(8,128)(2,1)}, u32[]{:S(2)}) %copy-start.5) | copy-done | bytes 65560
  7.2 0.0 copy-start.6
  7.2 0.7 copy-done.6
  7.9 0.0 copy-start.7
  7.9 0.7 copy-done.7
  8.6 73.7 %shard_map.100 = bf16[128,256]{1,0:T(8,128)(2,1)S(1)} custom-call(bf16[32,1024]{1,0:T(8,128)(2,1)S(1)} %copy-done.5, bf16[1024,128]{1,0:T(8,128)(2,1)S(1)} %copy-done.3, bf16[1024,128]{1,0:T(8,128)(2,1)S(1)} %copy-done.4, bf16[32,128]{1,0:T(8,128)(2,1)S(1)} %copy-done.6, bf16[32,128]{1,0:T(8,128)(2,1)S(1)} %copy-done.7, bf16[4,512,128]{2,1,0:T(8,128)(2,1)S(1)} %copy-done, ...), custom_call_target="tpu_custom_call" | custom-call | tf_op jit(solution)/shard_map/pallas_call | solution.py:432
  82.3 0.6 copy.12
  (1 shorter events, 0.0 us)
Async XLA Ops:
  0.0 0.7 copy-start.9
  0.7 0.7 copy-start.8
  1.3 1.0 %copy-start = (bf16[4,512,128]{2,1,0:T(8,128)(2,1)S(1)}, bf16[4,512,128]{2,1,0:T(8,128)(2,1)}, u32[]{:S(2)}) copy-start(bf16[4,512,128]{2,1,0:T(8,128)(2,1)} %ck_ref.1) | copy-start | bytes 1572868
  2.4 1.0 %copy-start.1 = (bf16[4,512,128]{2,1,0:T(8,128)(2,1)S(1)}, bf16[4,512,128]{2,1,0:T(8,128)(2,1)}, u32[]{:S(2)}) copy-start(bf16[4,512,128]{2,1,0:T(8,128)(2,1)} %cv_ref.1) | copy-start | bytes 1572868
  3.4 1.0 %copy-start.2 = (bf16[1024,256]{1,0:T(8,128)(2,1)S(1)}, bf16[1024,256]{1,0:T(8,128)(2,1)}, u32[]{:S(2)}) copy-start(bf16[1024,256]{1,0:T(8,128)(2,1)} %w_ref.1) | copy-start | bytes 1572868
  4.4 0.9 %copy-start.3 = (bf16[1024,128]{1,0:T(8,128)(2,1)S(1)}, bf16[1024,128]{1,0:T(8,128)(2,1)}, u32[]{:S(2)}) copy-start(bf16[1024,128]{1,0:T(8,128)(2,1)} %pk_ref.1) | copy-start | bytes 786436
  5.4 0.9 %copy-start.4 = (bf16[1024,128]{1,0:T(8,128)(2,1)S(1)}, bf16[1024,128]{1,0:T(8,128)(2,1)}, u32[]{:S(2)}) copy-start(bf16[1024,128]{1,0:T(8,128)(2,1)} %pv_ref.1) | copy-start | bytes 786436
  6.3 0.8 %copy-start.5 = (bf16[32,1024]{1,0:T(8,128)(2,1)S(1)}, bf16[32,1024]{1,0:T(8,128)(2,1)}, u32[]{:S(2)}) copy-start(bf16[32,1024]{1,0:T(8,128)(2,1)} %q_ref.1) | copy-start | bytes 196612
  7.2 0.7 copy-start.6
  7.9 0.7 copy-start.7

commit v2 on v1

v2 whole, which is shorter than its diff:
```python
import functools
import math

import jax
import jax.numpy as jnp
from jax import lax
from jax.experimental import pallas as pl
from jax.experimental.pallas import tpu as pltpu
from jax.sharding import PartitionSpec as P

HD = 128
QPG = 8
NY = 4
MESH = pl.DeviceIdType.MESH
SCALE2 = math.log2(math.e) / math.sqrt(HD)
LOG2E = math.log2(math.e)
LOW = -1e30
F32 = jnp.float32
BF16 = jnp.bfloat16


def kernel(
    nz,
    q_ref,
    pk_ref,
    pv_ref,
    nk_ref,
    nv_ref,
    ck_ref,
    cv_ref,
    rr_ref,
    cl_ref,
    w_ref,
    out_ref,
    kbuf,
    vbuf,
    qbuf,
    wbuf,
    ckb,
    cvb,
    nkb,
    nvb,
    rrs,
    cls,
    sca,
    scb,
    acc,
    mst,
    osend,
    orecv,
    att,
    proj,
    psend,
    precv,
    fsend,
    frecv,
    loc_sem,
    qs,
    qr,
    ks,
    kr,
    ws,
    wr,
    os_,
    or_,
    as_,
    ar,
    ps,
    pr,
    fs,
    fr,
):
    nt = nz
    rows = q_ref.shape[0]
    keys = pk_ref.shape[0]
    reqs, slots = ck_ref.shape[0], ck_ref.shape[1]
    depth, cols = w_ref.shape
    last = nz // 2
    s_idx = lax.axis_index("seq")
    t = lax.axis_index("tp")
    z = s_idx // NY
    y = s_idx % NY

    def at_z(v):
        return (lax.rem(v + 2 * nz, nz) * NY + y, t)

    def at_y(v):
        return (z * NY + lax.rem(v + 2 * NY, NY), t)

    def at_t(v):
        return (s_idx, lax.rem(v + 2 * nt, nt))

    def remote(src, dst, ssem, rsem, dev):
        return pltpu.make_async_remote_copy(
            src_ref=src,
            dst_ref=dst,
            send_sem=ssem,
            recv_sem=rsem,
            device_id=dev,
            device_id_type=MESH,
        )

    def greet(dev):
        pl.semaphore_signal(barrier, inc=1, device_id=dev, device_id_type=MESH)

    barrier = pltpu.get_barrier_semaphore()
    greet(at_y(y + 1))
    greet(at_y(y - 1))
    greet(at_z(z + 1))
    greet(at_z(z - 1))
    for i in range(1, nt):
        greet(at_t(t + i))

    local = [
        pltpu.make_async_copy(q_ref, qbuf.at[0], loc_sem.at[0]),
        pltpu.make_async_copy(ck_ref, ckb, loc_sem.at[1]),
        pltpu.make_async_copy(cv_ref, cvb, loc_sem.at[2]),
        pltpu.make_async_copy(nk_ref, nkb.at[pl.ds(0, rows)], loc_sem.at[3]),
        pltpu.make_async_copy(nv_ref, nvb.at[pl.ds(0, rows)], loc_sem.at[4]),
        pltpu.make_async_copy(rr_ref, rrs, loc_sem.at[5]),
        pltpu.make_async_copy(cl_ref, cls, loc_sem.at[6]),
        pltpu.make_async_copy(pk_ref, kbuf.at[0], loc_sem.at[7]),
        pltpu.make_async_copy(pv_ref, vbuf.at[0], loc_sem.at[8]),
        pltpu.make_async_copy(w_ref, wbuf.at[y], loc_sem.at[9]),
    ]
    for c in local:
        c.start()
    pl.semaphore_wait(barrier, nt + 3)

    lo, hi = pl.ds(0, keys // 2), pl.ds(keys // 2, keys // 2)
    ways = (at_y(y + 1), at_y(y - 1))
    place = (lo, hi)

    def kv_copy(stage, way, which):
        buf = (kbuf, vbuf)[which]
        whole = (pk_ref, pv_ref)[which]
        sem = (stage - 1) * 4 + way * 2 + which
        if stage == 1:
            src = whole.at[place[way]]
        elif stage == 2:
            src = whole.at[place[1 - way]]
        else:
            src = buf.at[1, place[way]]
        return remote(src, buf.at[stage, place[way]], ks.at[sem], kr.at[sem], ways[way])

    def kv_stage(stage, act):
        for which in range(2):
            for way in range(2):
                act(kv_copy(stage, way, which))

    kv_stage(1, lambda c: c.start())

    half = rows // 2
    halves = (pl.ds(0, half), pl.ds(half, half))
    zways = (at_z(z + 1), at_z(z - 1))

    def q_slot(way, k):
        return 2 * k - 1 if (way == 0 or k == last) else 2 * k

    def q_copy(way, k):
        dst = qbuf.at[q_slot(way, k)]
        src = q_ref if k == 1 else qbuf.at[q_slot(way, k - 1)]
        if k == last:
            src, dst = src.at[halves[way]], dst.at[halves[way]]
        return remote(src, dst, qs.at[way, k - 1], qr.at[way, k - 1], zways[way])

    for way in range(2):
        q_copy(way, 1).start()

    pad = nkb.shape[0]
    nkb[pl.ds(rows, pad - rows), :] = jnp.zeros((pad - rows, HD), BF16)
    nvb[pl.ds(rows, pad - rows), :] = jnp.zeros((pad - rows, HD), BF16)
    for c in local[:7]:
        c.wait()
    sub = lax.broadcasted_iota(jnp.int32, (rows, pad), 0)
    lane = lax.broadcasted_iota(jnp.int32, (rows, pad), 1)
    rr_col = jnp.zeros((rows, pad), jnp.int32)
    rr_row = jnp.zeros((rows, pad), jnp.int32)
    for r in range(rows):
        req = rrs[r] - s_idx * reqs
        rr_col = jnp.where(sub == r, req, rr_col)
        rr_row = jnp.where(lane == r, req, rr_row)

    def queries_of(i, first=0, heads=QPG):
        return jnp.concatenate(
            [qbuf[i, :, h * HD : (h + 1) * HD] for h in range(first, first + heads)], axis=0
        )

    def scores(q, k):
        return lax.dot_general(q, k, (((1,), (1,)), ((), ())), preferred_element_type=F32)

    def with_ones(v):
        return jnp.concatenate([v, jnp.ones_like(v)], axis=1)

    q_own = queries_of(0)
    parts = []
    for j in range(reqs):
        biases = [
            jnp.where((rr_col == j) & (lane + c * pad < cls[j]), 0.0, LOW).astype(F32)
            for c in range(slots // pad)
        ]
        bias = jnp.concatenate(biases, axis=1)
        parts.append(scores(q_own, ckb[j]) + jnp.concatenate([bias] * QPG, axis=0))
    bias = jnp.where((rr_row == rr_col) & (lane <= sub), 0.0, LOW).astype(F32)
    parts.append(scores(q_own, nkb[...]) + jnp.concatenate([bias] * QPG, axis=0))
    top = functools.reduce(jnp.maximum, [p.max(axis=1, keepdims=True) for p in parts])
    total = jnp.zeros((rows * QPG, 2 * HD), F32)
    for j, p in enumerate(parts):
        w = jnp.exp2((p - top) * SCALE2).astype(BF16)
        v = cvb[j] if j < reqs else nvb[...]
        total = total + jnp.dot(w, with_ones(v), preferred_element_type=F32)
    acc[0] = total
    mst[0] = jnp.broadcast_to(top, (rows * QPG, HD))
    for i in range(1, nz):
        acc[i] = jnp.zeros((rows * QPG, 2 * HD), F32)
        mst[i] = jnp.full((rows * QPG, HD), LOW, F32)

    kv_stage(2, lambda c: c.start())

    def fill(buf, blk, picks):
        q = jnp.concatenate([queries_of(i, f, n) for i, f, n in picks], axis=0)
        buf[...] = scores(q, kbuf[blk])

    def absorb(buf, blk, picks):
        ws_, alphas = [], []
        at = 0
        for i, f, n in picks:
            m = n * rows
            own = pl.ds(f * rows, m)
            chunks = [buf[at : at + m, c * HD : (c + 1) * HD] for c in range(keys // HD)]
            at += m
            m_old = mst[i, own]
            m_new = jnp.maximum(
                m_old, functools.reduce(jnp.maximum, chunks).max(axis=1, keepdims=True)
            )
            m2 = m_new * SCALE2
            ws_.append(
                jnp.concatenate([jnp.exp2(c * SCALE2 - m2).astype(BF16) for c in chunks], axis=1)
            )
            alphas.append(jnp.exp2(m_old * SCALE2 - m2))
            mst[i, own] = m_new
        o = jnp.dot(
            jnp.concatenate(ws_, axis=0), with_ones(vbuf[blk]), preferred_element_type=F32
        )
        at = 0
        for (i, f, n), alpha in zip(picks, alphas):
            m = n * rows
            own = pl.ds(f * rows, m)
            acc[i, own] = acc[i, own] * jnp.concatenate([alpha, alpha], axis=1) + o[at : at + m]
            at += m

    late = max(last - 2, 0)
    early = list(range(late))
    order = [(0, p) for p in early[:2]] + [(1, p) for p in early[:2]]
    for p in early[2:]:
        order += [(0, p), (1, p)]
    tail = list(range(late, last))
    if tail:
        order += [(0, tail[0]), (1, tail[0])]
    order += [(2, p) for p in early + tail[:1]]
    for p in tail[1:]:
        order += [(0, p), (1, p), (2, p)]
    need_q = {}
    for n, (b, p) in enumerate(order):
        need_q.setdefault(p, n)
    need_b = {b: min(n for n, o in enumerate(order) if o[0] == b) for b in (0, 1, 2)}

    def waits(n):
        def when(cond, act):
            if isinstance(n, int):
                if n == cond:
                    act()
            else:
                pl.when(n == cond)(act)

        def q_step(k):
            for way in range(2):
                q_copy(way, k).wait_recv()
                if k < last:
                    q_copy(way, k + 1).start()

        def own():
            for c in local[7:9]:
                c.wait()

        def blk1():
            kv_stage(1, lambda c: c.wait_recv())
            kv_stage(3, lambda c: c.start())

        when(need_b[0], own)
        for p in range(last):
            when(need_q[p], lambda p=p: q_step(p + 1))
        when(need_b[1], blk1)
        when(need_b[2], lambda: kv_stage(2, lambda c: c.wait_recv()))

    def tile(n):
        if isinstance(n, int):
            b, p = order[n]
        else:
            b = p = 0
            for m, (bb, pp) in enumerate(order):
                b = jnp.where(n == m, bb, b)
                p = jnp.where(n == m, pp, p)
        return b, [(2 * p, 0, QPG), (2 * p + 1, 0, QPG)]

    count = len(order)
    waits(0)
    fill(sca, *tile(0))

    def step(m, carry):
        for buf, other, n in ((sca, scb, 2 * m), (scb, sca, 2 * m + 1)):
            waits(n + 1)
            fill(other, *tile(n + 1))
            absorb(buf, *tile(n))
        return carry

    pairs = (count - 1) // 2
    lax.fori_loop(0, pairs, step, 0)
    rest = list(range(2 * pairs, count))
    bufs = (sca, scb)
    for n in rest:
        if n + 1 < count:
            waits(n + 1)
            fill(bufs[(n + 1) % 2], *tile(n + 1))
        absorb(bufs[n % 2], *tile(n))

    wlo, whi = pl.ds(0, depth // 2), pl.ds(depth // 2, depth // 2)
    wplace = (wlo, whi)
    origin = (lax.rem(y + NY - 1, NY), lax.rem(y + 1, NY))

    def w_copy(stage, way):
        sem = (stage - 1) * 2 + way
        if stage == 3:
            src = dst = wbuf.at[origin[way], wplace[way]]
        else:
            part = wplace[way] if stage == 1 else wplace[1 - way]
            src, dst = w_ref.at[part], wbuf.at[y, part]
        return remote(src, dst, ws.at[sem], wr.at[sem], ways[way])

    def w_stage(stage, act):
        for way in range(2):
            act(w_copy(stage, way))

    lane8 = lax.broadcasted_iota(jnp.int32, (8, HD), 1)
    groups = rows // 8
    hh = QPG // 2
    mh = hh * rows
    nslot = max(nz // 2, 1)

    def o_copy(c, i):
        if i % 2:
            dev = at_z(z - (i + 1) // 2)
        else:
            dev = at_z(z + i // 2)
        return remote(osend.at[c, i], orecv.at[c, i], os_.at[c, i], or_.at[c, i], dev)

    def finish(c, i):
        own = pl.ds(c * mh, mh)
        a = acc[i, own]
        l = a[:, HD:]
        osend[c, i, :mh] = (a[:, :HD] / l).astype(BF16)
        lse = mst[i, own] * SCALE2 + jnp.log(l) * LOG2E
        packed = jnp.zeros((8, HD), F32)
        for h in range(hh):
            for g in range(groups):
                r0 = h * rows + g * 8
                packed = jnp.where(lane8 == g * 8 + h, lse[r0 : r0 + 8, :], packed)
        p1 = packed.astype(BF16).astype(F32)
        p2 = (packed - p1).astype(BF16).astype(F32)
        p3 = (packed - p1 - p2).astype(BF16).astype(F32)
        p13 = p1 + pltpu.roll(p3, 32, 1)
        osend[c, i, mh:] = jnp.concatenate([p13, p2], axis=0).astype(BF16)

    finals = []
    for c in range(2):
        for g in range(nz // nslot - 1, -1, -1):
            finals.append((c, [(i, c * hh, hh) for i in range(g * nslot + nslot - 1, g * nslot - 1, -1)]))
    frows = nslot * mh
    fbufs = (sca.at[pl.ds(0, frows)], scb.at[pl.ds(0, frows)])

    kv_stage(3, lambda c: c.wait_recv())
    w_stage(1, lambda c: c.start())
    fill(fbufs[0], 3, finals[0][1])
    for n, (c, picks) in enumerate(finals):
        if n + 1 < len(finals):
            fill(fbufs[(n + 1) % 2], 3, finals[n + 1][1])
        absorb(fbufs[n % 2], 3, picks)
        for i, _, _ in picks:
            finish(c, i)
            if i > 0:
                o_copy(c, i).start()
        if n == 1:
            w_stage(2, lambda c: c.start())

    far_first = sorted(range(1, nz), key=lambda d: -min(d, nz - d))

    def a_copy(c, d):
        ref = att.at[c, z]
        return remote(ref, ref, as_.at[c, d], ar.at[c, d], at_z(z + d))

    def merge(c):
        for i in range(1, nz):
            o_copy(c, i).wait_recv()
        lses = []
        for i in range(nz):
            x = (osend if i == 0 else orecv)[c, i, mh:].astype(F32)
            lses.append(x[:8] + x[8:] + pltpu.roll(x[:8], HD - 32, 1))
        best = functools.reduce(jnp.maximum, lses)
        wts = [jnp.exp2(v - best) for v in lses]
        norm = functools.reduce(jnp.add, wts)
        wts = [v / norm for v in wts]
        for h in range(hh):
            tot = jnp.zeros((rows, HD), F32)
            for i in range(nz):
                o = (osend if i == 0 else orecv)[c, i, h * rows : (h + 1) * rows, :].astype(F32)
                col = jnp.concatenate(
                    [wts[i][:, g * 8 + h : g * 8 + h + 1] for g in range(groups)], axis=0
                )
                tot = tot + o * col
            att[c, z, :, h * HD : (h + 1) * HD] = tot.astype(BF16)
        for d in far_first:
            a_copy(c, d).start()

    merge(0)
    w_stage(1, lambda c: c.wait_recv())
    w_stage(3, lambda c: c.start())
    merge(1)

    local[9].wait()
    w_stage(2, lambda c: c.wait_recv())
    w_stage(3, lambda c: c.wait_recv())
    hd = depth // 2
    for c in range(2):
        for d in far_first:
            a_copy(c, d).wait_recv()
        a_all = att[c].reshape(nz * rows, hd)
        for j in range(NY):
            out = jnp.dot(a_all, wbuf[j, c * hd : (c + 1) * hd], preferred_element_type=F32)
            if c == 0:
                proj[:, j * cols : (j + 1) * cols] = out
            else:
                out = (out + proj[:, j * cols : (j + 1) * cols]).astype(BF16)
                psend[:, :, j * cols : (j + 1) * cols] = out.reshape(nz, rows, cols)

    def p_copy(e):
        dst_t = lax.rem(t + e, nt)
        return remote(psend.at[dst_t], precv.at[e], ps.at[e], pr.at[e], at_t(t + e))

    for e in range(1, nt):
        p_copy(e).start()
    tot = psend[t].astype(F32)
    for e in range(1, nt):
        p_copy(e).wait_recv()
        tot = tot + precv[e].astype(F32)
    tot = tot.astype(BF16)
    for j in range(NY):
        fsend[j] = tot[:, j * cols : (j + 1) * cols]

    def f_copy(e):
        dst_y = lax.rem(y + e, NY)
        return remote(fsend.at[dst_y], frecv.at[y], fs.at[e], fr.at[e], at_y(y + e))

    for e in range(1, NY):
        f_copy(e).start()
    frecv[y] = fsend[y]
    for e in range(1, NY):
        f_copy(e).wait_recv()
    out_ref[...] = frecv[...].reshape(NY * rows, cols)

    for way in range(2):
        for k in range(1, last + 1):
            q_copy(way, k).wait_send()
    for stage in (1, 2, 3):
        kv_stage(stage, lambda c: c.wait_send())
        w_stage(stage, lambda c: c.wait_send())
    for c in range(2):
        for i in range(1, nz):
            o_copy(c, i).wait_send()
            a_copy(c, i).wait_send()
    for e in range(1, nt):
        p_copy(e).wait_send()
    for e in range(1, NY):
        f_copy(e).wait_send()


def body(nz, q, pk, pv, nk, nv, ck, cv, rr, cl, w):
    rows = q.shape[0]
    feat = q.shape[1]
    keys = pk.shape[0]
    reqs, slots = ck.shape[0], ck.shape[1]
    depth, cols = w.shape
    m = rows * QPG
    wide = NY * cols
    last = nz // 2
    vm = pltpu.VMEM
    dma = pltpu.SemaphoreType.DMA
    any_spec = pl.BlockSpec(memory_space=pl.ANY)
    vmem_spec = pl.BlockSpec(memory_space=pltpu.VMEM)
    return pl.pallas_call(
        functools.partial(kernel, nz),
        out_shape=jax.ShapeDtypeStruct((NY * rows, cols), BF16),
        in_specs=[any_spec] * 10,
        out_specs=vmem_spec,
        scratch_shapes=[
            vm((NY, keys, HD), BF16),
            vm((NY, keys, HD), BF16),
            vm((nz, rows, feat), BF16),
            vm((NY, depth, cols), BF16),
            vm((reqs, slots, HD), BF16),
            vm((reqs, slots, HD), BF16),
            vm((HD, HD), BF16),
            vm((HD, HD), BF16),
            pltpu.SMEM((rows,), jnp.int32),
            pltpu.SMEM((reqs,), jnp.int32),
            vm((2 * m, keys), F32),
            vm((2 * m, keys), F32),
            vm((nz, m, 2 * HD), F32),
            vm((nz, m, HD), F32),
            vm((2, nz, m // 2 + 16, HD), BF16),
            vm((2, nz, m // 2 + 16, HD), BF16),
            vm((2, nz, rows, depth // 2), BF16),
            vm((nz * rows, wide), F32),
            vm((nz, rows, wide), BF16),
            vm((nz, rows, wide), BF16),
            vm((NY, rows, cols), BF16),
            vm((NY, rows, cols), BF16),
            dma((10,)),
            dma((2, last)),
            dma((2, last)),
            dma((12,)),
            dma((12,)),
            dma((6,)),
            dma((6,)),
            dma((2, nz)),
            dma((2, nz)),
            dma((2, nz)),
            dma((2, nz)),
            dma((nz,)),
            dma((nz,)),
            dma((NY,)),
            dma((NY,)),
        ],
        compiler_params=pltpu.CompilerParams(
            collective_id=0, has_side_effects=True, vmem_limit_bytes=60 * 1024 * 1024
        ),
    )(q, pk, pv, nk, nv, ck, cv, rr, cl, w)


def solution(mesh):
    nz = mesh.shape["seq"] // NY
    in_specs = (
        P("seq", "tp"),
        P("seq", "tp"),
        P("seq", "tp"),
        P("seq", "tp"),
        P("seq", "tp"),
        P("seq", None, "tp"),
        P("seq", None, "tp"),
        P("seq"),
        P("seq"),
        P("tp", "seq"),
    )
    return jax.shard_map(
        functools.partial(body, nz),
        mesh=mesh,
        in_specs=in_specs,
        out_specs=P("tp", "seq"),
        check_vma=False,
    )
```

time: 83.4 us -> 70.3 us (0.84)
  local copies, waits for them, and re-layouts: 9.19 us -> 1.47 us
  Pallas kernels: 73.7 us -> 68.7 us
    unnamed x21 -> x1, local copies, waits for them, and re-layouts: 9.19 us -> 1.47 us
    pallas_call x1, Pallas kernels: 73.7 us -> 68.7 us  [body(): pl.pallas_call(functools.partial(kernel, nz), out_shape=jax.ShapeDtypeStr...]
where the time goes in v2:
time: 70.3 us; the launch traced here: 70.2 us
  Pallas kernels  68.7 us (98%)
  local copies, waits for them, and re-layouts  1.47 us (2%)
    pallas_call x1, Pallas kernels, body(): pl.pallas_call(functools.partial(kernel, nz), out_shape=jax.ShapeDtypeStr...  68.7 us
    unnamed x1, local copies, waits for them, and re-layouts  1.47 us

profile of v2, /device:TPU:1, one launch (start us, length us, event | category | flops | bytes accessed | tf_op | source)
XLA Modules:
  0.0 70.2 jit_solution(9482384931235035508)
XLA Ops:
  0.0 68.7 %shard_map.100 = bf16[128,256]{1,0:T(8,128)(2,1)} custom-call(bf16[32,1024]{1,0:T(8,128)(2,1)} %q_ref.1, bf16[1024,128]{1,0:T(8,128)(2,1)} %pk_ref.1, bf16[1024,128]{1,0:T(8,128)(2,1)} %pv_ref.1, bf16[32,128]{1,0:T(8,128)(2,1)} %nk_ref.1, bf16[32,128]{1,0:T(8,128)(2,1)} %nv_ref.1, bf16[4,512,128]{2,1,0:T(8,128)(2,1)} %ck_ref.1, bf16[4,512,128]{2,1,0:T(8,128)(2,1)} %cv_ref.1, ...), custom_call_target="tpu_custom_call" | custom-call | tf_op jit(solution)/shard_map/pallas_call | solution.py:499
  68.7 1.5 %copy.12 = bf16[128,256]{1,0:T(8,128)(2,1)} copy(bf16[128,256]{1,0:T(8,128)(2,1)} %shard_map.100) | data formatting | bytes 131072

commit v3 on v2

--- a/solution.py
+++ b/solution.py
@@ -49,7 +49,6 @@
     osend,
     orecv,
     att,
-    proj,
     psend,
     precv,
     fsend,
@@ -123,8 +122,6 @@
         pltpu.make_async_copy(pv_ref, vbuf.at[0], loc_sem.at[8]),
         pltpu.make_async_copy(w_ref, wbuf.at[y], loc_sem.at[9]),
     ]
-    for c in local:
-        c.start()
     pl.semaphore_wait(barrier, nt + 3)
 
     lo, hi = pl.ds(0, keys // 2), pl.ds(keys // 2, keys // 2)
@@ -166,6 +163,8 @@
 
     for way in range(2):
         q_copy(way, 1).start()
+    for c in local:
+        c.start()
 
     pad = nkb.shape[0]
     nkb[pl.ds(rows, pad - rows), :] = jnp.zeros((pad - rows, HD), BF16)
@@ -181,10 +180,18 @@
         rr_col = jnp.where(sub == r, req, rr_col)
         rr_row = jnp.where(lane == r, req, rr_row)
 
-    def queries_of(i, first=0, heads=QPG):
+    def queries_of(i, first=0, parts=2):
         return jnp.concatenate(
-            [qbuf[i, :, h * HD : (h + 1) * HD] for h in range(first, first + heads)], axis=0
+            [
+                qbuf[i, c * half : (c + 1) * half, h * HD : (h + 1) * HD]
+                for c in range(first, first + parts)
+                for h in range(QPG)
+            ],
+            axis=0,
         )
+
+    def per_head(bias):
+        return jnp.concatenate([bias[:half]] * QPG + [bias[half:]] * QPG, axis=0)
 
     def scores(q, k):
         return lax.dot_general(q, k, (((1,), (1,)), ((), ())), preferred_element_type=F32)
@@ -200,9 +207,9 @@
             for c in range(slots // pad)
         ]
         bias = jnp.concatenate(biases, axis=1)
-        parts.append(scores(q_own, ckb[j]) + jnp.concatenate([bias] * QPG, axis=0))
+        parts.append(scores(q_own, ckb[j]) + per_head(bias))
     bias = jnp.where((rr_row == rr_col) & (lane <= sub), 0.0, LOW).astype(F32)
-    parts.append(scores(q_own, nkb[...]) + jnp.concatenate([bias] * QPG, axis=0))
+    parts.append(scores(q_own, nkb[...]) + per_head(bias))
     top = functools.reduce(jnp.maximum, [p.max(axis=1, keepdims=True) for p in parts])
     total = jnp.zeros((rows * QPG, 2 * HD), F32)
     for j, p in enumerate(parts):
@@ -215,7 +222,7 @@
         acc[i] = jnp.zeros((rows * QPG, 2 * HD), F32)
         mst[i] = jnp.full((rows * QPG, HD), LOW, F32)
 
-    kv_stage(2, lambda c: c.start())
+    mh = half * QPG
 
     def fill(buf, blk, picks):
         q = jnp.concatenate([queries_of(i, f, n) for i, f, n in picks], axis=0)
@@ -225,8 +232,8 @@
         ws_, alphas = [], []
         at = 0
         for i, f, n in picks:
-            m = n * rows
-            own = pl.ds(f * rows, m)
+            m = n * mh
+            own = pl.ds(f * mh, m)
             chunks = [buf[at : at + m, c * HD : (c + 1) * HD] for c in range(keys // HD)]
             at += m
             m_old = mst[i, own]
@@ -244,8 +251,8 @@
         )
         at = 0
         for (i, f, n), alpha in zip(picks, alphas):
-            m = n * rows
-            own = pl.ds(f * rows, m)
+            m = n * mh
+            own = pl.ds(f * mh, m)
             acc[i, own] = acc[i, own] * jnp.concatenate([alpha, alpha], axis=1) + o[at : at + m]
             at += m
 
@@ -301,11 +308,12 @@
             for m, (bb, pp) in enumerate(order):
                 b = jnp.where(n == m, bb, b)
                 p = jnp.where(n == m, pp, p)
-        return b, [(2 * p, 0, QPG), (2 * p + 1, 0, QPG)]
+        return b, [(2 * p, 0, 2), (2 * p + 1, 0, 2)]
 
     count = len(order)
     waits(0)
     fill(sca, *tile(0))
+    kv_stage(2, lambda c: c.start())
 
     def step(m, carry):
         for buf, other, n in ((sca, scb, 2 * m), (scb, sca, 2 * m + 1)):
@@ -342,9 +350,7 @@
             act(w_copy(stage, way))
 
     lane8 = lax.broadcasted_iota(jnp.int32, (8, HD), 1)
-    groups = rows // 8
-    hh = QPG // 2
-    mh = hh * rows
+    groups = half // 8
     nslot = max(nz // 2, 1)
 
     def o_copy(c, i):
@@ -359,12 +365,16 @@
         a = acc[i, own]
         l = a[:, HD:]
         osend[c, i, :mh] = (a[:, :HD] / l).astype(BF16)
-        lse = mst[i, own] * SCALE2 + jnp.log(l) * LOG2E
-        packed = jnp.zeros((8, HD), F32)
-        for h in range(hh):
+        m = mst[i, own]
+        top_of = jnp.zeros((8, HD), F32)
+        sum_of = jnp.ones((8, HD), F32)
+        for h in range(QPG):
             for g in range(groups):
-                r0 = h * rows + g * 8
-                packed = jnp.where(lane8 == g * 8 + h, lse[r0 : r0 + 8, :], packed)
+                r0 = h * half + g * 8
+                pick = lane8 == g * 8 + h
+                top_of = jnp.where(pick, m[r0 : r0 + 8, :], top_of)
+                sum_of = jnp.where(pick, l[r0 : r0 + 8, :], sum_of)
+        packed = top_of * SCALE2 + jnp.log(sum_of) * LOG2E
         p1 = packed.astype(BF16).astype(F32)
         p2 = (packed - p1).astype(BF16).astype(F32)
         p3 = (packed - p1 - p2).astype(BF16).astype(F32)
@@ -374,7 +384,8 @@
     finals = []
     for c in range(2):
         for g in range(nz // nslot - 1, -1, -1):
-            finals.append((c, [(i, c * hh, hh) for i in range(g * nslot + nslot - 1, g * nslot - 1, -1)]))
+            picks = range(g * nslot + nslot - 1, g * nslot - 1, -1)
+            finals.append((c, [(i, c, 1) for i in picks]))
     frows = nslot * mh
     fbufs = (sca.at[pl.ds(0, frows)], scb.at[pl.ds(0, frows)])
 
@@ -409,10 +420,10 @@
         wts = [jnp.exp2(v - best) for v in lses]
         norm = functools.reduce(jnp.add, wts)
         wts = [v / norm for v in wts]
-        for h in range(hh):
-            tot = jnp.zeros((rows, HD), F32)
+        for h in range(QPG):
+            tot = jnp.zeros((half, HD), F32)
             for i in range(nz):
-                o = (osend if i == 0 else orecv)[c, i, h * rows : (h + 1) * rows, :].astype(F32)
+                o = (osend if i == 0 else orecv)[c, i, h * half : (h + 1) * half, :].astype(F32)
                 col = jnp.concatenate(
                     [wts[i][:, g * 8 + h : g * 8 + h + 1] for g in range(groups)], axis=0
                 )
@@ -429,43 +440,41 @@
     local[9].wait()
     w_stage(2, lambda c: c.wait_recv())
     w_stage(3, lambda c: c.wait_recv())
-    hd = depth // 2
+
+    def p_copy(c, e):
+        dst_t = lax.rem(t + e, nt)
+        return remote(psend.at[c, dst_t], precv.at[c, e], ps.at[c, e], pr.at[c, e], at_t(t + e))
+
     for c in range(2):
         for d in far_first:
             a_copy(c, d).wait_recv()
-        a_all = att[c].reshape(nz * rows, hd)
+        a_all = att[c].reshape(nz * half, depth)
         for j in range(NY):
-            out = jnp.dot(a_all, wbuf[j, c * hd : (c + 1) * hd], preferred_element_type=F32)
-            if c == 0:
-                proj[:, j * cols : (j + 1) * cols] = out
-            else:
-                out = (out + proj[:, j * cols : (j + 1) * cols]).astype(BF16)
-                psend[:, :, j * cols : (j + 1) * cols] = out.reshape(nz, rows, cols)
-
-    def p_copy(e):
-        dst_t = lax.rem(t + e, nt)
-        return remote(psend.at[dst_t], precv.at[e], ps.at[e], pr.at[e], at_t(t + e))
-
-    for e in range(1, nt):
-        p_copy(e).start()
-    tot = psend[t].astype(F32)
-    for e in range(1, nt):
-        p_copy(e).wait_recv()
-        tot = tot + precv[e].astype(F32)
-    tot = tot.astype(BF16)
-    for j in range(NY):
-        fsend[j] = tot[:, j * cols : (j + 1) * cols]
-
-    def f_copy(e):
+            out = jnp.dot(a_all, wbuf[j], preferred_element_type=F32).astype(BF16)
+            psend[c, :, :, j * cols : (j + 1) * cols] = out.reshape(nz, half, cols)
+        for e in range(1, nt):
+            p_copy(c, e).start()
+
+    def f_copy(c, e):
         dst_y = lax.rem(y + e, NY)
-        return remote(fsend.at[dst_y], frecv.at[y], fs.at[e], fr.at[e], at_y(y + e))
-
-    for e in range(1, NY):
-        f_copy(e).start()
-    frecv[y] = fsend[y]
-    for e in range(1, NY):
-        f_copy(e).wait_recv()
-    out_ref[...] = frecv[...].reshape(NY * rows, cols)
+        return remote(fsend.at[c, dst_y], frecv.at[c, y], fs.at[c, e], fr.at[c, e], at_y(y + e))
+
+    for c in range(2):
+        tot = psend[c, t].astype(F32)
+        for e in range(1, nt):
+            p_copy(c, e).wait_recv()
+            tot = tot + precv[c, e].astype(F32)
+        tot = tot.astype(BF16)
+        for j in range(NY):
+            fsend[c, j] = tot[:, j * cols : (j + 1) * cols]
+        for e in range(1, NY):
+            f_copy(c, e).start()
+        frecv[c, y] = fsend[c, y]
+    for c in range(2):
+        for e in range(1, NY):
+            f_copy(c, e).wait_recv()
+        for j in range(NY):
+            out_ref[j * rows + c * half : j * rows + (c + 1) * half, :] = frecv[c, j]
 
     for way in range(2):
         for k in range(1, last + 1):
@@ -477,10 +486,10 @@
         for i in range(1, nz):
             o_copy(c, i).wait_send()
             a_copy(c, i).wait_send()
-    for e in range(1, nt):
-        p_copy(e).wait_send()
-    for e in range(1, NY):
-        f_copy(e).wait_send()
+        for e in range(1, nt):
+            p_copy(c, e).wait_send()
+        for e in range(1, NY):
+            f_copy(c, e).wait_send()
 
 
 def body(nz, q, pk, pv, nk, nv, ck, cv, rr, cl, w):
@@ -518,12 +527,11 @@
             vm((nz, m, HD), F32),
             vm((2, nz, m // 2 + 16, HD), BF16),
             vm((2, nz, m // 2 + 16, HD), BF16),
-            vm((2, nz, rows, depth // 2), BF16),
-            vm((nz * rows, wide), F32),
-            vm((nz, rows, wide), BF16),
-            vm((nz, rows, wide), BF16),
-            vm((NY, rows, cols), BF16),
-            vm((NY, rows, cols), BF16),
+            vm((2, nz, rows // 2, depth), BF16),
+            vm((2, nz, rows // 2, wide), BF16),
+            vm((2, nz, rows // 2, wide), BF16),
+            vm((2, NY, rows // 2, cols), BF16),
+            vm((2, NY, rows // 2, cols), BF16),
             dma((10,)),
             dma((2, last)),
             dma((2, last)),
@@ -535,10 +543,10 @@
             dma((2, nz)),
             dma((2, nz)),
             dma((2, nz)),
-            dma((nz,)),
-            dma((nz,)),
-            dma((NY,)),
-            dma((NY,)),
+            dma((2, nz)),
+            dma((2, nz)),
+            dma((2, NY)),
+            dma((2, NY)),
         ],
         compiler_params=pltpu.CompilerParams(
             collective_id=0, has_side_effects=True, vmem_limit_bytes=60 * 1024 * 1024

time: 70.3 us -> 67.4 us (0.959)
  Pallas kernels: 68.7 us -> 65.8 us
    pallas_call x1, Pallas kernels: 68.7 us -> 65.8 us  [body(): pl.pallas_call(functools.partial(kernel, nz), out_shape=jax.ShapeDtypeStr...]
where the time goes in v3:
time: 67.4 us; the launch traced here: 67.2 us
  Pallas kernels  65.8 us (98%)
  local copies, waits for them, and re-layouts  1.47 us (2%)
    pallas_call x1, Pallas kernels, body(): pl.pallas_call(functools.partial(kernel, nz), out_shape=jax.ShapeDtypeStr...  65.8 us
    unnamed x1, local copies, waits for them, and re-layouts  1.47 us

profile of v3, /device:TPU:1, one launch (start us, length us, event | category | flops | bytes accessed | tf_op | source)
XLA Modules:
  0.0 67.2 jit_solution(16999395856068696002)
XLA Ops:
  0.0 65.8 %shard_map.100 = bf16[128,256]{1,0:T(8,128)(2,1)} custom-call(bf16[32,1024]{1,0:T(8,128)(2,1)} %q_ref.1, bf16[1024,128]{1,0:T(8,128)(2,1)} %pk_ref.1, bf16[1024,128]{1,0:T(8,128)(2,1)} %pv_ref.1, bf16[32,128]{1,0:T(8,128)(2,1)} %nk_ref.1, bf16[32,128]{1,0:T(8,128)(2,1)} %nv_ref.1, bf16[4,512,128]{2,1,0:T(8,128)(2,1)} %ck_ref.1, bf16[4,512,128]{2,1,0:T(8,128)(2,1)} %cv_ref.1, ...), custom_call_target="tpu_custom_call" | custom-call | tf_op jit(solution)/shard_map/pallas_call | solution.py:508
  65.8 1.5 %copy.12 = bf16[128,256]{1,0:T(8,128)(2,1)} copy(bf16[128,256]{1,0:T(8,128)(2,1)} %shard_map.100) | data formatting | bytes 131072

commit v4 on v3

--- a/solution.py
+++ b/solution.py
@@ -48,6 +48,8 @@
     mst,
     osend,
     orecv,
+    lsend,
+    lrecv,
     att,
     psend,
     precv,
@@ -62,6 +64,8 @@
     wr,
     os_,
     or_,
+    ls,
+    lr,
     as_,
     ar,
     ps,
@@ -163,22 +167,8 @@
 
     for way in range(2):
         q_copy(way, 1).start()
-    for c in local:
+    for c in (local[0], local[7], local[8]):
         c.start()
-
-    pad = nkb.shape[0]
-    nkb[pl.ds(rows, pad - rows), :] = jnp.zeros((pad - rows, HD), BF16)
-    nvb[pl.ds(rows, pad - rows), :] = jnp.zeros((pad - rows, HD), BF16)
-    for c in local[:7]:
-        c.wait()
-    sub = lax.broadcasted_iota(jnp.int32, (rows, pad), 0)
-    lane = lax.broadcasted_iota(jnp.int32, (rows, pad), 1)
-    rr_col = jnp.zeros((rows, pad), jnp.int32)
-    rr_row = jnp.zeros((rows, pad), jnp.int32)
-    for r in range(rows):
-        req = rrs[r] - s_idx * reqs
-        rr_col = jnp.where(sub == r, req, rr_col)
-        rr_row = jnp.where(lane == r, req, rr_row)
 
     def queries_of(i, first=0, parts=2):
         return jnp.concatenate(
@@ -199,26 +189,7 @@
     def with_ones(v):
         return jnp.concatenate([v, jnp.ones_like(v)], axis=1)
 
-    q_own = queries_of(0)
-    parts = []
-    for j in range(reqs):
-        biases = [
-            jnp.where((rr_col == j) & (lane + c * pad < cls[j]), 0.0, LOW).astype(F32)
-            for c in range(slots // pad)
-        ]
-        bias = jnp.concatenate(biases, axis=1)
-        parts.append(scores(q_own, ckb[j]) + per_head(bias))
-    bias = jnp.where((rr_row == rr_col) & (lane <= sub), 0.0, LOW).astype(F32)
-    parts.append(scores(q_own, nkb[...]) + per_head(bias))
-    top = functools.reduce(jnp.maximum, [p.max(axis=1, keepdims=True) for p in parts])
-    total = jnp.zeros((rows * QPG, 2 * HD), F32)
-    for j, p in enumerate(parts):
-        w = jnp.exp2((p - top) * SCALE2).astype(BF16)
-        v = cvb[j] if j < reqs else nvb[...]
-        total = total + jnp.dot(w, with_ones(v), preferred_element_type=F32)
-    acc[0] = total
-    mst[0] = jnp.broadcast_to(top, (rows * QPG, HD))
-    for i in range(1, nz):
+    for i in range(nz):
         acc[i] = jnp.zeros((rows * QPG, 2 * HD), F32)
         mst[i] = jnp.full((rows * QPG, HD), LOW, F32)
 
@@ -287,12 +258,14 @@
                     q_copy(way, k + 1).start()
 
         def own():
-            for c in local[7:9]:
+            for c in (local[0], local[7], local[8]):
                 c.wait()
 
         def blk1():
-            kv_stage(1, lambda c: c.wait_recv())
-            kv_stage(3, lambda c: c.start())
+            for which in range(2):
+                for way in range(2):
+                    kv_copy(1, way, which).wait_recv()
+                    kv_copy(3, way, which).start()
 
         when(need_b[0], own)
         for p in range(last):
@@ -314,6 +287,8 @@
     waits(0)
     fill(sca, *tile(0))
     kv_stage(2, lambda c: c.start())
+    for c in local[1:7] + local[9:]:
+        c.start()
 
     def step(m, carry):
         for buf, other, n in ((sca, scb, 2 * m), (scb, sca, 2 * m + 1)):
@@ -351,20 +326,35 @@
 
     lane8 = lax.broadcasted_iota(jnp.int32, (8, HD), 1)
     groups = half // 8
-    nslot = max(nz // 2, 1)
+
+    staged = nz == 8
+
+    def o_dest(c, i):
+        if staged and i == 7:
+            return at_z(z - 2) if c == 0 else at_z(z + 2)
+        if staged and i > 4:
+            return at_z(z - 1) if i == 5 else at_z(z + 1)
+        return at_z(z - (i + 1) // 2) if i % 2 else at_z(z + i // 2)
 
     def o_copy(c, i):
-        if i % 2:
-            dev = at_z(z - (i + 1) // 2)
-        else:
-            dev = at_z(z + i // 2)
-        return remote(osend.at[c, i], orecv.at[c, i], os_.at[c, i], or_.at[c, i], dev)
+        return remote(osend.at[c, i], orecv.at[c, i], os_.at[c, i], or_.at[c, i], o_dest(c, i))
+
+    def l_copy(c, i):
+        return remote(lsend.at[c, i], lrecv.at[c, i], ls.at[c, i], lr.at[c, i], o_dest(c, i))
+
+    def o_start(c, i):
+        o_copy(c, i).start()
+        l_copy(c, i).start()
+
+    def o_wait(c, i):
+        o_copy(c, i).wait_recv()
+        l_copy(c, i).wait_recv()
 
     def finish(c, i):
         own = pl.ds(c * mh, mh)
         a = acc[i, own]
         l = a[:, HD:]
-        osend[c, i, :mh] = (a[:, :HD] / l).astype(BF16)
+        osend[c, i] = (a[:, :HD] / l).astype(BF16)
         m = mst[i, own]
         top_of = jnp.zeros((8, HD), F32)
         sum_of = jnp.ones((8, HD), F32)
@@ -375,33 +365,78 @@
                 top_of = jnp.where(pick, m[r0 : r0 + 8, :], top_of)
                 sum_of = jnp.where(pick, l[r0 : r0 + 8, :], sum_of)
         packed = top_of * SCALE2 + jnp.log(sum_of) * LOG2E
-        p1 = packed.astype(BF16).astype(F32)
-        p2 = (packed - p1).astype(BF16).astype(F32)
-        p3 = (packed - p1 - p2).astype(BF16).astype(F32)
-        p13 = p1 + pltpu.roll(p3, 32, 1)
-        osend[c, i, mh:] = jnp.concatenate([p13, p2], axis=0).astype(BF16)
+        rolled = pltpu.roll(packed, 0, 1, stride=16, stride_axis=0)
+        lsend[c, i] = jnp.sum(rolled, axis=0, keepdims=True)
 
     finals = []
-    for c in range(2):
-        for g in range(nz // nslot - 1, -1, -1):
-            picks = range(g * nslot + nslot - 1, g * nslot - 1, -1)
-            finals.append((c, [(i, c, 1) for i in picks]))
-    frows = nslot * mh
-    fbufs = (sca.at[pl.ds(0, frows)], scb.at[pl.ds(0, frows)])
-
-    kv_stage(3, lambda c: c.wait_recv())
-    w_stage(1, lambda c: c.start())
-    fill(fbufs[0], 3, finals[0][1])
+    for top_slot, low_slot in ((nz, nz // 2), (nz // 2, 0)):
+        for c in range(2):
+            finals.append((c, [(i, c, 1) for i in range(top_slot - 1, low_slot - 1, -1)]))
+
+    def part(n):
+        return (sca, scb)[n % 2].at[pl.ds(0, len(finals[n][1]) * mh)]
+
+    for way in range(2):
+        kv_copy(3, way, 0).wait_recv()
+    fill(part(0), 3, finals[0][1])
+    for way in range(2):
+        kv_copy(3, way, 1).wait_recv()
     for n, (c, picks) in enumerate(finals):
         if n + 1 < len(finals):
-            fill(fbufs[(n + 1) % 2], 3, finals[n + 1][1])
-        absorb(fbufs[n % 2], 3, picks)
+            fill(part(n + 1), 3, finals[n + 1][1])
+        absorb(part(n), 3, picks)
         for i, _, _ in picks:
-            finish(c, i)
             if i > 0:
-                o_copy(c, i).start()
-        if n == 1:
+                finish(c, i)
+                if not (staged and i in (3, 4)):
+                    o_start(c, i)
+        if n == 0:
+            w_stage(1, lambda c: c.start())
+        if n == 2:
             w_stage(2, lambda c: c.start())
+
+    pad = nkb.shape[0]
+    nkb[pl.ds(rows, pad - rows), :] = jnp.zeros((pad - rows, HD), BF16)
+    nvb[pl.ds(rows, pad - rows), :] = jnp.zeros((pad - rows, HD), BF16)
+    for c in local[1:7]:
+        c.wait()
+    sub = lax.broadcasted_iota(jnp.int32, (rows, pad), 0)
+    lane = lax.broadcasted_iota(jnp.int32, (rows, pad), 1)
+    rr_col = jnp.zeros((rows, pad), jnp.int32)
+    rr_row = jnp.zeros((rows, pad), jnp.int32)
+    for r in range(rows):
+        req = rrs[r] - s_idx * reqs
+        rr_col = jnp.where(sub == r, req, rr_col)
+        rr_row = jnp.where(lane == r, req, rr_row)
+
+    q_own = queries_of(0)
+    parts = []
+    for j in range(reqs):
+        biases = [
+            jnp.where((rr_col == j) & (lane + c * pad < cls[j]), 0.0, LOW).astype(F32)
+            for c in range(slots // pad)
+        ]
+        bias = jnp.concatenate(biases, axis=1)
+        parts.append(scores(q_own, ckb[j]) + per_head(bias))
+    bias = jnp.where((rr_row == rr_col) & (lane <= sub), 0.0, LOW).astype(F32)
+    parts.append(scores(q_own, nkb[...]) + per_head(bias))
+    top = functools.reduce(jnp.maximum, [p.max(axis=1, keepdims=True) for p in parts])
+    total = jnp.zeros((rows * QPG, 2 * HD), F32)
+    for j, p in enumerate(parts):
+        w = jnp.exp2((p - top) * SCALE2).astype(BF16)
+        v = cvb[j] if j < reqs else nvb[...]
+        total = total + jnp.dot(w, with_ones(v), preferred_element_type=F32)
+    top = jnp.broadcast_to(top, (rows * QPG, HD))
+    m_old = mst[0]
+    m_new = jnp.maximum(m_old, top)
+    keep = jnp.exp2((m_old - m_new) * SCALE2)
+    add = jnp.exp2((top - m_new) * SCALE2)
+    acc[0] = acc[0] * jnp.concatenate([keep, keep], axis=1) + total * jnp.concatenate(
+        [add, add], axis=1
+    )
+    mst[0] = m_new
+    for c in range(2):
+        finish(c, 0)
 
     far_first = sorted(range(1, nz), key=lambda d: -min(d, nz - d))
 
@@ -409,33 +444,64 @@
         ref = att.at[c, z]
         return remote(ref, ref, as_.at[c, d], ar.at[c, d], at_z(z + d))
 
-    def merge(c):
-        for i in range(1, nz):
-            o_copy(c, i).wait_recv()
-        lses = []
-        for i in range(nz):
-            x = (osend if i == 0 else orecv)[c, i, mh:].astype(F32)
-            lses.append(x[:8] + x[8:] + pltpu.roll(x[:8], HD - 32, 1))
+    sub8 = lax.broadcasted_iota(jnp.int32, (8, HD), 0)
+
+    def spread(row):
+        row = jnp.broadcast_to(row, (8, HD))
+        out = row
+        for k in range(1, 8):
+            out = jnp.where(sub8 == k, pltpu.roll(row, HD - 16 * k, 1), out)
+        return out
+
+    def weights(c, sources):
+        lses = [lsend[c, i] if own else lrecv[c, i] for own, i in sources]
         best = functools.reduce(jnp.maximum, lses)
         wts = [jnp.exp2(v - best) for v in lses]
         norm = functools.reduce(jnp.add, wts)
-        wts = [v / norm for v in wts]
+        return [spread(v / norm) for v in wts], best + jnp.log(norm) * LOG2E
+
+    def blend(c, sources, wts, h):
+        tot = jnp.zeros((half, HD), F32)
+        for (own, i), w in zip(sources, wts):
+            o = (osend if own else orecv)[c, i, h * half : (h + 1) * half, :].astype(F32)
+            col = jnp.concatenate(
+                [w[:, g * 8 + h : g * 8 + h + 1] for g in range(groups)], axis=0
+            )
+            tot = tot + o * col
+        return tot.astype(BF16)
+
+    def join(c):
+        o_wait(c, 5)
+        o_wait(c, 6)
+        o_wait(c, 7)
+        for i, extra in ((3, 5), (4, 6)):
+            sources = [(True, i), (False, extra)]
+            if i == 3 + c:
+                sources.append((False, 7))
+            wts, lse = weights(c, sources)
+            for h in range(QPG):
+                osend[c, i, h * half : (h + 1) * half, :] = blend(c, sources, wts, h)
+            lsend[c, i] = lse
+            o_start(c, i)
+
+    def merge(c):
+        arriving = range(1, 5) if staged else range(1, nz)
+        for i in arriving:
+            o_wait(c, i)
+        sources = [(True, 0)] + [(False, i) for i in arriving]
+        wts, _ = weights(c, sources)
         for h in range(QPG):
-            tot = jnp.zeros((half, HD), F32)
-            for i in range(nz):
-                o = (osend if i == 0 else orecv)[c, i, h * half : (h + 1) * half, :].astype(F32)
-                col = jnp.concatenate(
-                    [wts[i][:, g * 8 + h : g * 8 + h + 1] for g in range(groups)], axis=0
-                )
-                tot = tot + o * col
-            att[c, z, :, h * HD : (h + 1) * HD] = tot.astype(BF16)
+            att[c, z, :, h * HD : (h + 1) * HD] = blend(c, sources, wts, h)
         for d in far_first:
             a_copy(c, d).start()
 
+    if staged:
+        join(0)
+        join(1)
     merge(0)
+    merge(1)
     w_stage(1, lambda c: c.wait_recv())
     w_stage(3, lambda c: c.start())
-    merge(1)
 
     local[9].wait()
     w_stage(2, lambda c: c.wait_recv())
@@ -458,6 +524,18 @@
     def f_copy(c, e):
         dst_y = lax.rem(y + e, NY)
         return remote(fsend.at[c, dst_y], frecv.at[c, y], fs.at[c, e], fr.at[c, e], at_y(y + e))
+
+    for way in range(2):
+        for k in range(1, last + 1):
+            q_copy(way, k).wait_send()
+    for stage in (1, 2, 3):
+        kv_stage(stage, lambda c: c.wait_send())
+        w_stage(stage, lambda c: c.wait_send())
+    for c in range(2):
+        for i in range(1, nz):
+            o_copy(c, i).wait_send()
+            l_copy(c, i).wait_send()
+            a_copy(c, i).wait_send()
 
     for c in range(2):
         tot = psend[c, t].astype(F32)
@@ -476,16 +554,7 @@
         for j in range(NY):
             out_ref[j * rows + c * half : j * rows + (c + 1) * half, :] = frecv[c, j]
 
-    for way in range(2):
-        for k in range(1, last + 1):
-            q_copy(way, k).wait_send()
-    for stage in (1, 2, 3):
-        kv_stage(stage, lambda c: c.wait_send())
-        w_stage(stage, lambda c: c.wait_send())
     for c in range(2):
-        for i in range(1, nz):
-            o_copy(c, i).wait_send()
-            a_copy(c, i).wait_send()
         for e in range(1, nt):
             p_copy(c, e).wait_send()
         for e in range(1, NY):
@@ -525,8 +594,10 @@
             vm((2 * m, keys), F32),
             vm((nz, m, 2 * HD), F32),
             vm((nz, m, HD), F32),
-            vm((2, nz, m // 2 + 16, HD), BF16),
-            vm((2, nz, m // 2 + 16, HD), BF16),
+            vm((2, nz, m // 2, HD), BF16),
+            vm((2, nz, m // 2, HD), BF16),
+            vm((2, nz, 1, HD), F32),
+            vm((2, nz, 1, HD), F32),
             vm((2, nz, rows // 2, depth), BF16),
             vm((2, nz, rows // 2, wide), BF16),
             vm((2, nz, rows // 2, wide), BF16),
@@ -539,6 +610,8 @@
             dma((12,)),
             dma((6,)),
             dma((6,)),
+            dma((2, nz)),
+            dma((2, nz)),
             dma((2, nz)),
             dma((2, nz)),
             dma((2, nz)),

time: 67.4 us -> 64 us (0.950)
  Pallas kernels: 65.8 us -> 62.4 us
    pallas_call x1, Pallas kernels: 65.8 us -> 62.4 us  [body(): pl.pallas_call(functools.partial(kernel, nz), out_shape=jax.ShapeDtypeStr...]
where the time goes in v4:
time: 64 us; the launch traced here: 63.9 us
  Pallas kernels  62.4 us (98%)
  local copies, waits for them, and re-layouts  1.47 us (2%)
    pallas_call x1, Pallas kernels, body(): pl.pallas_call(functools.partial(kernel, nz), out_shape=jax.ShapeDtypeStr...  62.4 us
    unnamed x1, local copies, waits for them, and re-layouts  1.47 us

profile of v4, /device:TPU:1, one launch (start us, length us, event | category | flops | bytes accessed | tf_op | source)
XLA Modules:
  0.0 63.9 jit_solution(15533062990321417335)
XLA Ops:
  0.0 62.4 %shard_map.100 = bf16[128,256]{1,0:T(8,128)(2,1)} custom-call(bf16[32,1024]{1,0:T(8,128)(2,1)} %q_ref.1, bf16[1024,128]{1,0:T(8,128)(2,1)} %pk_ref.1, bf16[1024,128]{1,0:T(8,128)(2,1)} %pv_ref.1, bf16[32,128]{1,0:T(8,128)(2,1)} %nk_ref.1, bf16[32,128]{1,0:T(8,128)(2,1)} %nv_ref.1, bf16[4,512,128]{2,1,0:T(8,128)(2,1)} %ck_ref.1, bf16[4,512,128]{2,1,0:T(8,128)(2,1)} %cv_ref.1, ...), custom_call_target="tpu_custom_call" | custom-call | tf_op jit(solution)/shard_map/pallas_call | solution.py:577
  62.4 1.5 %copy.12 = bf16[128,256]{1,0:T(8,128)(2,1)} copy(bf16[128,256]{1,0:T(8,128)(2,1)} %shard_map.100) | data formatting | bytes 131072

commit v5 on v4

--- a/solution.py
+++ b/solution.py
@@ -111,6 +111,9 @@
     greet(at_y(y - 1))
     greet(at_z(z + 1))
     greet(at_z(z - 1))
+    if nz == 8:
+        greet(at_z(z + 2))
+        greet(at_z(z - 2))
     for i in range(1, nt):
         greet(at_t(t + i))
 
@@ -126,7 +129,7 @@
         pltpu.make_async_copy(pv_ref, vbuf.at[0], loc_sem.at[8]),
         pltpu.make_async_copy(w_ref, wbuf.at[y], loc_sem.at[9]),
     ]
-    pl.semaphore_wait(barrier, nt + 3)
+    pl.semaphore_wait(barrier, nt + (5 if nz == 8 else 3))
 
     lo, hi = pl.ds(0, keys // 2), pl.ds(keys // 2, keys // 2)
     ways = (at_y(y + 1), at_y(y - 1))
@@ -153,20 +156,22 @@
 
     half = rows // 2
     halves = (pl.ds(0, half), pl.ds(half, half))
-    zways = (at_z(z + 1), at_z(z - 1))
+    reach = 2 if nz == 8 else 1
 
     def q_slot(way, k):
         return 2 * k - 1 if (way == 0 or k == last) else 2 * k
 
     def q_copy(way, k):
         dst = qbuf.at[q_slot(way, k)]
-        src = q_ref if k == 1 else qbuf.at[q_slot(way, k - 1)]
+        src = q_ref if k <= reach else qbuf.at[q_slot(way, reach)]
+        step = k if k <= reach else k - reach
         if k == last:
             src, dst = src.at[halves[way]], dst.at[halves[way]]
-        return remote(src, dst, qs.at[way, k - 1], qr.at[way, k - 1], zways[way])
-
-    for way in range(2):
-        q_copy(way, 1).start()
+        return remote(src, dst, qs.at[way, k - 1], qr.at[way, k - 1], at_z(z + step if way == 0 else z - step))
+
+    for k in range(1, min(reach, last) + 1):
+        for way in range(2):
+            q_copy(way, k).start()
     for c in (local[0], local[7], local[8]):
         c.start()
 
@@ -254,8 +259,10 @@
         def q_step(k):
             for way in range(2):
                 q_copy(way, k).wait_recv()
-                if k < last:
-                    q_copy(way, k + 1).start()
+            if k == reach:
+                for far in range(last, reach, -1):
+                    for way in range(2):
+                        q_copy(way, far).start()
 
         def own():
             for c in (local[0], local[7], local[8]):
@@ -471,13 +478,12 @@
         return tot.astype(BF16)
 
     def join(c):
-        o_wait(c, 5)
-        o_wait(c, 6)
-        o_wait(c, 7)
-        for i, extra in ((3, 5), (4, 6)):
-            sources = [(True, i), (False, extra)]
+        for i in (4 - c, 3 + c):
+            sources = [(True, i), (False, i + 2)]
             if i == 3 + c:
                 sources.append((False, 7))
+            for _, extra in sources[1:]:
+                o_wait(c, extra)
             wts, lse = weights(c, sources)
             for h in range(QPG):
                 osend[c, i, h * half : (h + 1) * half, :] = blend(c, sources, wts, h)
@@ -518,7 +524,7 @@
         for j in range(NY):
             out = jnp.dot(a_all, wbuf[j], preferred_element_type=F32).astype(BF16)
             psend[c, :, :, j * cols : (j + 1) * cols] = out.reshape(nz, half, cols)
-        for e in range(1, nt):
+        for e in sorted(range(1, nt), key=lambda e: -min(e, nt - e)):
             p_copy(c, e).start()
 
     def f_copy(c, e):

time: 64 us -> 63.3 us (0.989)
  Pallas kernels: 62.4 us -> 61.7 us
    pallas_call x1, Pallas kernels: 62.4 us -> 61.7 us  [body(): pl.pallas_call(functools.partial(kernel, nz), out_shape=jax.ShapeDtypeStr...]
where the time goes in v5:
time: 63.3 us; the launch traced here: 63.2 us
  Pallas kernels  61.7 us (97%)
  local copies, waits for them, and re-layouts  1.47 us (2%)
    pallas_call x1, Pallas kernels, body(): pl.pallas_call(functools.partial(kernel, nz), out_shape=jax.ShapeDtypeStr...  61.7 us
    unnamed x1, local copies, waits for them, and re-layouts  1.47 us

profile of v5, /device:TPU:1, one launch (start us, length us, event | category | flops | bytes accessed | tf_op | source)
XLA Modules:
  0.0 63.2 jit_solution(14820552208668952185)
XLA Ops:
  0.0 61.7 %shard_map.100 = bf16[128,256]{1,0:T(8,128)(2,1)} custom-call(bf16[32,1024]{1,0:T(8,128)(2,1)} %q_ref.1, bf16[1024,128]{1,0:T(8,128)(2,1)} %pk_ref.1, bf16[1024,128]{1,0:T(8,128)(2,1)} %pv_ref.1, bf16[32,128]{1,0:T(8,128)(2,1)} %nk_ref.1, bf16[32,128]{1,0:T(8,128)(2,1)} %nv_ref.1, bf16[4,512,128]{2,1,0:T(8,128)(2,1)} %ck_ref.1, bf16[4,512,128]{2,1,0:T(8,128)(2,1)} %cv_ref.1, ...), custom_call_target="tpu_custom_call" | custom-call | tf_op jit(solution)/shard_map/pallas_call | solution.py:583
  61.7 1.5 %copy.12 = bf16[128,256]{1,0:T(8,128)(2,1)} copy(bf16[128,256]{1,0:T(8,128)(2,1)} %shard_map.100) | data formatting | bytes 131072

commit v6 on v5

--- a/solution.py
+++ b/solution.py
@@ -72,6 +72,7 @@
     pr,
     fs,
     fr,
+    heard,
 ):
     nt = nz
     rows = q_ref.shape[0]
@@ -114,8 +115,12 @@
     if nz == 8:
         greet(at_z(z + 2))
         greet(at_z(z - 2))
-    for i in range(1, nt):
-        greet(at_t(t + i))
+    partner = t + 1 - 2 * lax.rem(t, 2)
+    greet(at_t(partner))
+    if nt == 8:
+        greet(at_t(t + 2))
+        greet(at_t(t - 2))
+        greet(at_t(partner + 4))
 
     local = [
         pltpu.make_async_copy(q_ref, qbuf.at[0], loc_sem.at[0]),
@@ -129,7 +134,7 @@
         pltpu.make_async_copy(pv_ref, vbuf.at[0], loc_sem.at[8]),
         pltpu.make_async_copy(w_ref, wbuf.at[y], loc_sem.at[9]),
     ]
-    pl.semaphore_wait(barrier, nt + (5 if nz == 8 else 3))
+    pl.semaphore_wait(barrier, 10 if nz == 8 else 5)
 
     lo, hi = pl.ds(0, keys // 2), pl.ds(keys // 2, keys // 2)
     ways = (at_y(y + 1), at_y(y - 1))
@@ -174,6 +179,7 @@
             q_copy(way, k).start()
     for c in (local[0], local[7], local[8]):
         c.start()
+    pl.semaphore_signal(heard, inc=1, device_id=at_t(partner), device_id_type=MESH)
 
     def queries_of(i, first=0, parts=2):
         return jnp.concatenate(
@@ -506,6 +512,7 @@
         join(1)
     merge(0)
     merge(1)
+    pl.semaphore_wait(heard, 1)
     w_stage(1, lambda c: c.wait_recv())
     w_stage(3, lambda c: c.start())
 
@@ -626,6 +633,7 @@
             dma((2, nz)),
             dma((2, NY)),
             dma((2, NY)),
+            pltpu.SemaphoreType.REGULAR,
         ],
         compiler_params=pltpu.CompilerParams(
             collective_id=0, has_side_effects=True, vmem_limit_bytes=60 * 1024 * 1024

time: 63.3 us -> 63.6 us (level)
  no operation moved by 1% of the time
where the time goes in v6:
time: 63.6 us; the launch traced here: 63.5 us
  Pallas kernels  62 us (97%)
  local copies, waits for them, and re-layouts  1.47 us (2%)
    pallas_call x1, Pallas kernels, body(): pl.pallas_call(functools.partial(kernel, nz), out_shape=jax.ShapeDtypeStr...  62 us
    unnamed x1, local copies, waits for them, and re-layouts  1.47 us

profile of v6, /device:TPU:1, one launch (start us, length us, event | category | flops | bytes accessed | tf_op | source)
XLA Modules:
  0.0 63.5 jit_solution(256371089366449244)
XLA Ops:
  0.0 62.0 %shard_map.100 = bf16[128,256]{1,0:T(8,128)(2,1)} custom-call(bf16[32,1024]{1,0:T(8,128)(2,1)} %q_ref.1, bf16[1024,128]{1,0:T(8,128)(2,1)} %pk_ref.1, bf16[1024,128]{1,0:T(8,128)(2,1)} %pv_ref.1, bf16[32,128]{1,0:T(8,128)(2,1)} %nk_ref.1, bf16[32,128]{1,0:T(8,128)(2,1)} %nv_ref.1, bf16[4,512,128]{2,1,0:T(8,128)(2,1)} %ck_ref.1, bf16[4,512,128]{2,1,0:T(8,128)(2,1)} %cv_ref.1, ...), custom_call_target="tpu_custom_call" | custom-call | tf_op jit(solution)/shard_map/pallas_call | solution.py:590
  62.0 1.5 %copy.12 = bf16[128,256]{1,0:T(8,128)(2,1)} copy(bf16[128,256]{1,0:T(8,128)(2,1)} %shard_map.100) | data formatting | bytes 131072
